TPU v7x, 512 devices: a whole 4x8x8 slice. The times are simulated.
512 devices in a mesh: group: 16 (over y, core), dev: 32 (over z, x).
Axes of the slice: x: 4, y: 8, z: 8, core: 2. Of those that a mesh axis runs over, the one named last changes fastest.
Arguments:
- queries: bfloat16 [4096, 2, 8192], P(('group', 'dev')), may hold values from -50 to 50
- new_keys: bfloat16 [4096, 2, 1024], P(('group', 'dev')), may hold values from -6 to 6
- new_values: bfloat16 [4096, 2, 1024], P(('group', 'dev')), may hold values from -24 to 24
- suffix_keys: bfloat16 [4096, 32, 1024], P(('group', 'dev')), may hold values from -6 to 6
- suffix_values: bfloat16 [4096, 32, 1024], P(('group', 'dev')), may hold values from -24 to 24
- suffix_lengths: int32 [4096], P(('group', 'dev')), may hold values from 1 to 32
- root_keys: bfloat16 [1024, 1024], P('group'), may hold values from -6 to 6
- root_values: bfloat16 [1024, 1024], P('group'), may hold values from -24 to 24
- prefix_keys: bfloat16 [1024, 256, 1024], P(('group', 'dev')), may hold values from -6 to 6
- prefix_values: bfloat16 [1024, 256, 1024], P(('group', 'dev')), may hold values from -24 to 24
- prefix_lengths: int32 [1024], P(('group', 'dev')), may hold values from 2 to 256
- owner_map: int32 [16, 64], P('group'), may hold values from 0 to 63, as said below
- block_lists: int32 [4096, 2], P(('group', 'dev')), may hold values from 0 to 63, as said below
Outputs:
- attended: bfloat16 [4096, 2, 8192], P(('group', 'dev'))
Inputs may be any that keep to these rules, and one draw needn't show every extreme that they name: Each row is a permutation of 0 to 63: block b of group g is kept by the device owner_map[g, b] // 2 of that group along dev, in its local slot owner_map[g, b] % 2. `block_lists`: block ids of the request's own group; the 2 blocks of one request are distinct. Of the 16 blocks named in one device's rows, at most 2 are kept by any one device, and in every group some device keeps exactly 2 of those of every device of the group.
All inputs are finite; a program needn't handle non-finite values.
Results may differ from a plain program's by a relative error of at most 0.0075.
Values may be sent and summed in bfloat16 or wider, within the bound.
A program may use at most 64 MiB of HBM per device.

v0:
```python
import math

import jax
import jax.numpy as jnp
from jax import lax
from jax.sharding import PartitionSpec as P

HEADS = 64
KV_HEADS = 8
HEAD = 128
REFS = 2


def head_layout(query_rows):
    row_count = query_rows.shape[0]
    per_kv = HEADS // KV_HEADS
    split_rows = query_rows.reshape(row_count, 2, KV_HEADS, per_kv, HEAD)
    return split_rows.transpose(2, 0, 1, 3, 4).reshape(KV_HEADS, row_count * 2 * per_kv, HEAD)


def request_layout(head_major, row_count):
    per_kv = HEADS // KV_HEADS
    trailing = head_major.shape[2:]
    shaped = head_major.reshape((KV_HEADS, row_count, 2, per_kv) + trailing)
    axes_order = (1, 2, 0, 3) + tuple(range(4, 4 + len(trailing)))
    return shaped.transpose(axes_order).reshape((row_count, 2, HEADS) + trailing)


def serve_slots(asked, asked_slots, prefix_keys, prefix_values, prefix_lengths):
    score_scale = 1.0 / math.sqrt(HEAD)
    per_kv = HEADS // KV_HEADS
    senders = asked_slots.shape[0]
    depth = asked_slots.shape[1]
    slot_count = senders * depth
    owned = prefix_keys.shape[0]
    block_len = prefix_keys.shape[1]
    token_count = owned * block_len
    query_heads = head_layout(asked.reshape(slot_count, 2, HEADS * HEAD))
    key_heads = prefix_keys.reshape(token_count, KV_HEADS, HEAD).transpose(1, 0, 2)
    value_heads = prefix_values.reshape(token_count, KV_HEADS, HEAD).transpose(1, 0, 2)
    token_block = jnp.arange(token_count, dtype=jnp.int32) // block_len
    token_within = jnp.arange(token_count, dtype=jnp.int32) % block_len
    block_match = token_block[:, None] == jnp.arange(owned, dtype=jnp.int32)[None, :]
    token_limit = jnp.sum(jnp.where(block_match, prefix_lengths[None, :], 0), axis=1)
    chosen = jnp.maximum(asked_slots.reshape(slot_count), 0)
    valid_slot = (token_block[None, :] == chosen[:, None]) & (token_within < token_limit)[None, :]
    valid_rows = jnp.repeat(valid_slot, 2 * per_kv, axis=0)

    def one_head(operands):
        head_queries, head_keys, head_values = operands
        scores = (
            jnp.einsum("qd,ld->ql", head_queries, head_keys, preferred_element_type=jnp.float32)
            * score_scale
        )
        scores = jnp.where(valid_rows, scores, -jnp.inf)
        highest = jnp.max(scores, axis=1)
        weights = jnp.exp(scores - highest[:, None])
        totals = jnp.sum(weights, axis=1)
        summed = jnp.dot(
            weights.astype(jnp.bfloat16), head_values, preferred_element_type=jnp.float32
        )
        answer = (summed / totals[:, None]).astype(jnp.bfloat16)
        return (answer, highest + jnp.log(totals))

    answers, log_totals = lax.map(one_head, (query_heads, key_heads, value_heads))
    answers = request_layout(answers, slot_count).reshape(senders, depth, 2, HEADS * HEAD)
    log_totals = request_layout(log_totals, slot_count).reshape(senders, depth, 2, HEADS)
    return (answers, log_totals)


def shards(
    queries,
    new_keys,
    new_values,
    suffix_keys,
    suffix_values,
    suffix_lengths,
    root_keys,
    root_values,
    prefix_keys,
    prefix_values,
    prefix_lengths,
    owner_map,
    block_lists,
):
    score_scale = 1.0 / math.sqrt(HEAD)
    per_kv = HEADS // KV_HEADS
    per_request = 2 * per_kv
    requests = queries.shape[0]
    owners = lax.axis_size("dev")
    pair_count = requests * REFS
    capacity = pair_count // owners + 2
    slot_count = owners * capacity
    block_total = owner_map.shape[1]
    pool_size = prefix_keys.shape[0]
    query_heads = head_layout(queries)
    by_request = query_heads.reshape(KV_HEADS, requests, per_request, HEAD)
    past_len = suffix_keys.shape[1]
    past_keys = suffix_keys.reshape(requests, past_len, KV_HEADS, HEAD)
    past_values = suffix_values.reshape(requests, past_len, KV_HEADS, HEAD)
    fresh_keys = new_keys.reshape(requests, 2, KV_HEADS, HEAD)
    fresh_values = new_values.reshape(requests, 2, KV_HEADS, HEAD)
    past_scores = (
        jnp.einsum("krqd,rlkd->krql", by_request, past_keys, preferred_element_type=jnp.float32)
        * score_scale
    )
    past_valid = jnp.arange(past_len, dtype=jnp.int32)[None, :] < suffix_lengths[:, None]
    past_scores = jnp.where(past_valid[None, :, None, :], past_scores, -jnp.inf)
    fresh_scores = (
        jnp.einsum("krqd,rjkd->krqj", by_request, fresh_keys, preferred_element_type=jnp.float32)
        * score_scale
    )
    fresh_valid = (
        jnp.arange(2, dtype=jnp.int32)[None, :]
        <= (jnp.arange(per_request, dtype=jnp.int32) // per_kv)[:, None]
    )
    fresh_scores = jnp.where(fresh_valid[None, None, :, :], fresh_scores, -jnp.inf)
    highest = jnp.maximum(jnp.max(past_scores, axis=3), jnp.max(fresh_scores, axis=3))
    past_weights = jnp.exp(past_scores - highest[..., None])
    fresh_weights = jnp.exp(fresh_scores - highest[..., None])
    totals = jnp.sum(past_weights, axis=3) + jnp.sum(fresh_weights, axis=3)
    summed = jnp.einsum(
        "krql,rlkd->krqd",
        past_weights.astype(jnp.bfloat16),
        past_values,
        preferred_element_type=jnp.float32,
    )
    summed = summed + jnp.einsum(
        "krqj,rjkd->krqd",
        fresh_weights.astype(jnp.bfloat16),
        fresh_values,
        preferred_element_type=jnp.float32,
    )
    running = (
        highest.reshape(KV_HEADS, -1),
        totals.reshape(KV_HEADS, -1),
        summed.reshape(KV_HEADS, -1, HEAD),
    )
    highest_old, totals_old, summed_old = running
    part_keys = lax.all_gather(root_keys, "group", axis=0, tiled=True)
    part_values = lax.all_gather(root_values, "group", axis=0, tiled=True)
    length = part_keys.shape[0]
    part_keys = part_keys.reshape(length, KV_HEADS, HEAD)
    part_values = part_values.reshape(length, KV_HEADS, HEAD)
    scores = (
        jnp.einsum("kqd,lkd->kql", query_heads, part_keys, preferred_element_type=jnp.float32)
        * score_scale
    )
    highest_new = jnp.maximum(highest_old, jnp.max(scores, axis=2))
    weights = jnp.exp(scores - highest_new[..., None])
    factor = jnp.exp(highest_old - highest_new)
    totals_new = totals_old * factor + jnp.sum(weights, axis=2)
    summed_new = summed_old * factor[..., None] + jnp.einsum(
        "kql,lkd->kqd",
        weights.astype(jnp.bfloat16),
        part_values,
        preferred_element_type=jnp.float32,
    )
    running = (highest_new, totals_new, summed_new)
    owner_table = owner_map[0]
    flat_blocks = block_lists.reshape(pair_count)
    block_hits = flat_blocks[:, None] == jnp.arange(block_total, dtype=jnp.int32)[None, :]
    global_slot = jnp.sum(jnp.where(block_hits, owner_table[None, :], 0), axis=1)
    target = global_slot // pool_size
    local_slot = global_slot % pool_size
    target_hits = (target[:, None] == jnp.arange(owners, dtype=jnp.int32)[None, :]).astype(
        jnp.int32
    )
    earlier = jnp.cumsum(target_hits, axis=0) - target_hits
    rank_within = jnp.sum(earlier * target_hits, axis=1)
    position = target * capacity + rank_within
    slot_hits = position[None, :] == jnp.arange(slot_count, dtype=jnp.int32)[:, None]
    occupied = jnp.any(slot_hits, axis=1)
    slot_pair = jnp.sum(
        jnp.where(slot_hits, jnp.arange(pair_count, dtype=jnp.int32)[None, :], 0), axis=1
    )
    send_queries = jnp.where(
        occupied[:, None, None], queries[slot_pair // REFS], jnp.zeros((), jnp.bfloat16)
    )
    send_queries = send_queries.reshape(owners, capacity, 2, HEADS * HEAD)
    send_slots = jnp.where(occupied, local_slot[slot_pair], -1).reshape(owners, capacity)
    asked, asked_slots = (
        lax.all_to_all(send_queries, "dev", split_axis=0, concat_axis=0, tiled=True),
        lax.all_to_all(send_slots, "dev", split_axis=0, concat_axis=0, tiled=True),
    )
    answers, log_totals = serve_slots(
        asked, asked_slots, prefix_keys, prefix_values, prefix_lengths
    )
    back_answers, back_logs = (
        lax.all_to_all(
            answers.astype(jnp.float32), "dev", split_axis=0, concat_axis=0, tiled=True
        ).astype(answers.dtype),
        lax.all_to_all(log_totals, "dev", split_axis=0, concat_axis=0, tiled=True),
    )
    pair_answers = back_answers.reshape(slot_count, 2, HEADS * HEAD)[position]
    pair_logs = back_logs.reshape(slot_count, 2, HEADS)[position]
    pair_answers = pair_answers.reshape(requests, REFS, 2, HEADS, HEAD).astype(jnp.float32)
    pair_logs = pair_logs.reshape(requests, REFS, 2, HEADS)
    local_highest = request_layout(running[0], requests)
    local_totals = request_layout(running[1], requests)
    local_summed = request_layout(running[2], requests)
    largest = jnp.maximum(local_highest, jnp.max(pair_logs, axis=1))
    local_share = jnp.exp(local_highest - largest)
    pair_share = jnp.exp(pair_logs - largest[:, None])
    numerator = local_summed * local_share[..., None] + jnp.sum(
        pair_share[..., None] * pair_answers, axis=1
    )
    denominator = local_totals * local_share + jnp.sum(pair_share, axis=1)
    return (
        (numerator / denominator[..., None]).reshape(requests, 2, HEADS * HEAD).astype(jnp.bfloat16)
    )


def solution(mesh):
    return jax.shard_map(
        shards,
        mesh=mesh,
        in_specs=(
            P(("group", "dev"), None, None),
            P(("group", "dev"), None, None),
            P(("group", "dev"), None, None),
            P(("group", "dev"), None, None),
            P(("group", "dev"), None, None),
            P(("group", "dev")),
            P("group", None),
            P("group", None),
            P(("group", "dev"), None, None),
            P(("group", "dev"), None, None),
            P(("group", "dev")),
            P("group", None),
            P(("group", "dev"), None),
        ),
        out_specs=P(("group", "dev"), None, None),
        check_vma=False,
    )
```

profile of v0, /device:TPU:12, one launch (start us, length us, event | category | flops | bytes accessed | tf_op | source)
XLA Modules:
  0.0 222.6 jit_solution(6436637629256837498)
XLA Ops:
  10.3 13.4 %all-to-all-start.1 = ((s32[32,1,2]{2,1,0:T(1,128)}), s32[32,1,2]{2,1,0:T(1,128)S(1)}, u32[]{:S(2)}, u32[]{:S(2)}) async-start(s32[32,1,2]{2,1,0:T(1,128)} %bitcast.18), calls=%async_computation.1 | async-start | bytes 32768 | tf_op jit(solution)/shard_map/all_to_all | solution.py:184
  24.6 6.1 %gather_fusion = bf16[64,2,8192]{2,1,0:T(2,128)(2,1)S(1)} fusion(bf16[8,2,8192]{2,1,0:T(2,128)(2,1)S(1)} %copy-done.1, s32[1024]{0:T(1024)S(1)} %get-tuple-element.132), kind=kCustom, calls=%fused_computation | custom fusion | bytes 4194560 | tf_op jit(solution)/shard_map/gather | solution.py:178
  30.7 3.1 %broadcast_select_fusion = bf16[32,2,2,8192]{3,2,1,0:T(2,128)(2,1)} fusion(bf16[32,2,2,8192]{3,2,1,0:T(2,128)(2,1)S(1)} %bitcast.176, pred[32,2]{1,0:T(8,128)(4,1)S(1)} %broadcast_in_dim.141), kind=kLoop, calls=%fused_computation.25 | loop fusion | flops 1048576 | bytes 4194368 | tf_op jit(solution)/shard_map/jit(_where)/select_n | solution.py:177
  33.8 9.8 %all-to-all-start = ((bf16[32,2,2,8192]{3,2,1,0:T(2,128)(2,1)}), bf16[32,2,2,8192]{3,2,1,0:T(2,128)(2,1)S(1)}, u32[]{:S(2)}, u32[]{:S(2)}) async-start(bf16[32,2,2,8192]{3,2,1,0:T(2,128)(2,1)} %broadcast_select_fusion), calls=%async_computation | async-start | bytes 4194304 | tf_op jit(solution)/shard_map/all_to_all | solution.py:183
  49.2 43.7 %all-to-all-done = bf16[32,2,2,8192]{3,2,1,0:T(2,128)(2,1)S(1)} async-done(((bf16[32,2,2,8192]{3,2,1,0:T(2,128)(2,1)}), bf16[32,2,2,8192]{3,2,1,0:T(2,128)(2,1)S(1)}, u32[]{:S(2)}, u32[]{:S(2)}) %all-to-all-start) | async-done | bytes 2097184 | tf_op jit(solution)/shard_map/all_to_all | solution.py:183
  92.9 2.8 %reshape_reshape.11 = bf16[64,2,8,8,128]{4,3,2,1,0:T(8,128)(2,1)} reshape(bf16[32,2,2,8192]{3,2,1,0:T(2,128)(2,1)S(1)} %all-to-all-done) | data formatting | bytes 4194304 | tf_op jit(solution)/shard_map/reshape;reshape | solution.py:17
  95.7 3.3 %copy.127 = bf16[8,64,2,8,128]{4,3,2,1,0:T(8,128)(2,1)} copy(bf16[8,64,2,8,128]{4,3,0,2,1:T(8,128)(2,1)} %bitcast.177) | data formatting | bytes 4194304 | tf_op jit(solution)/shard_map/transpose | solution.py:18
  99.0 38.9 %while.13 = (s32[]{:T(128)}, bf16[8,1024,128]{2,1,0:T(8,128)(2,1)}, f32[8,1024]{1,0:T(8,128)S(1)}, bf16[8,1024,128]{2,1,0:T(8,128)(2,1)}, bf16[8,512,128]{2,1,0:...) while((s32[]{:T(128)}, bf16[8,1024,128]{2,1,0:T(8,128)(2,1)}, ...), condition=%wide.region_12.13_spmd.clone, body=%wide.region_9.12_spmd.clone.sunk | while | flops 272366592 | bytes 9250913 | solution.py:65
  101.8 2.1 fusion.89
  111.5 2.2 fusion.89
  116.4 2.2 fusion.89
  135.8 2.2 fusion.89
  140.0 6.3 %all-to-all-start.2 = ((f32[32,1,256]{2,1,0:T(1,128)}), f32[32,1,256]{2,1,0:T(1,128)S(1)}, u32[]{:S(2)}, u32[]{:S(2)}) async-start(f32[32,1,256]{2,1,0:T(1,128)} %reshape.535), calls=%async_computation.2 | async-start | bytes 65536 | tf_op jit(solution)/shard_map/all_to_all | solution.py:193
  146.6 2.2 copy.185
  150.9 3.3 %all-to-all-done.2 = f32[32,1,256]{2,1,0:T(1,128)S(1)} async-done(((f32[32,1,256]{2,1,0:T(1,128)}), f32[32,1,256]{2,1,0:T(1,128)S(1)}, u32[]{:S(2)}, u32[]{:S(2)}) %all-to-all-start.2) | async-done | bytes 32800 | tf_op jit(solution)/shard_map/all_to_all | solution.py:193
  154.7 6.6 %all-to-all-start.3 = ((bf16[32,2,2,8192]{3,2,1,0:T(2,128)(2,1)}), bf16[32,2,2,8192]{3,2,1,0:T(2,128)(2,1)}, u32[]{:S(2)}, u32[]{:S(2)}) async-start(bf16[32,2,2,8192]{3,2,1,0:T(2,128)(2,1)} %reshape.489), calls=%async_computation.3 | async-start | bytes 4194304 | tf_op jit(solution)/shard_map/all_to_all | solution.py:190
  164.8 2.9 %copy.120 = bf16[1024,1024]{0,1:T(8,128)(2,1)S(1)} copy(bf16[1024,1024]{1,0:T(8,128)(2,1)} %all-gather.3.cloned.1.call-done) | data formatting | bytes 4194304 | tf_op jit(solution)/shard_map/all_gather | solution.py:140
  167.7 2.6 %multiply_reduce_fusion = (f32[8,128]{1,0:T(8,128)S(1)}, f32[8,128,1024]{2,1,0:T(8,128)}) fusion(bf16[8,128,128]{2,1,0:T(8,128)(2,1)S(1)} %bitcast.186, bf16[1024,8,128]{0,2,1:T(8,128)(2,1)S(1)} %bitcast.179), kind=kOutput, calls=%fused_computation.26 | convolution fusion | flops 270531584 | bytes 6557696 | tf_op jit(solution)/shard_map/kqd,lkd->kql/dot_general | solution.py:146
  170.5 3.1 %fusion.17 = f32[8,128]{1,0:T(8,128)S(1)} fusion(f32[8,128,1024]{2,1,0:T(8,128)} %get-tuple-element.130, f32[8,128]{1,0:T(8,128)S(1)} %get-tuple-element.112), kind=kLoop, calls=%fused_computation.27 | loop fusion | flops 3144704 | bytes 4202496 | tf_op jit(solution)/shard_map/reduce_sum | solution.py:152
  174.1 2.9 %copy.122 = bf16[1024,1024]{0,1:T(8,128)(2,1)S(1)} copy(bf16[1024,1024]{1,0:T(8,128)(2,1)} %all-gather.5.cloned.1.call-done) | data formatting | bytes 4194304 | tf_op jit(solution)/shard_map/all_gather | solution.py:141
  177.1 3.2 %fusion.23 = f32[8,128,128]{2,1,0:T(8,128)S(1)} fusion(f32[8,128,128]{2,1,0:T(8,128)S(1)} %bitcast_multiply_fusion, bf16[1024,8,128]{0,2,1:T(8,128)(2,1)S(1)} %bitcast.175, f32[8,128,1024]{2,1,0:T(8,128)} %get-tuple-element.130, f32[8,128]{1,0:T(8,128)S(1)} %get-tuple-element.112), kind=kOutput, calls=%fused_computation.33 | convolution fusion | flops 271712256 | bytes 7344128 | tf_op jit(solution)/shard_map/kql,lkd->kqd/dot_general | solution.py:153
  184.7 24.5 %all-to-all-done.3 = bf16[32,2,2,8192]{3,2,1,0:T(2,128)(2,1)} async-done(((bf16[32,2,2,8192]{3,2,1,0:T(2,128)(2,1)}), bf16[32,2,2,8192]{3,2,1,0:T(2,128)(2,1)}, u32[]{:S(2)}, u32[]{:S(2)}) %all-to-all-start.3) | async-done | bytes 2097184 | tf_op jit(solution)/shard_map/all_to_all | solution.py:190
  209.2 3.3 %gather_fusion.3 = bf16[16,2,8192]{2,1,0:T(2,128)(2,1)S(1)} fusion(bf16[64,2,8192]{2,1,0:T(2,128)(2,1)} %bitcast.27, s32[1024]{0:T(1024)} %pad_clamp_fusion), kind=kCustom, calls=%fused_computation.3 | custom fusion | bytes 1048640 | tf_op jit(solution)/shard_map/gather | solution.py:195
  213.5 2.2 %fusion.33 = bf16[8,2,8192]{2,1,0:T(2,128)(2,1)} fusion(f32[8,2,8192]{2,1,0:T(2,128)S(1)} %div.75, f32[8,2,8192]{2,1,0:T(2,128)S(1)} %reduce_sum.108, f32[8,2,8192]{2,1,0:T(2,128)S(1)} %reshape.478, f32[8,2,8192]{2,1,0:T(2,128)} %mul.90), kind=kLoop, calls=%fused_computation.47 | loop fusion | flops 524288 | bytes 2359296 | tf_op jit(solution)/shard_map/convert_element_type | solution.py:210
  (161 shorter events, 54.5 us)
Async XLA Ops:
  6.5 157.6 %copy-start = (bf16[8,32,1024]{2,1,0:T(8,128)(2,1)S(1)}, bf16[8,32,1024]{2,1,0:T(8,128)(2,1)}, u32[]{:S(2)}) copy-start(bf16[8,32,1024]{2,1,0:T(8,128)(2,1)} %param.19) | copy-start | bytes 1572868
  6.5 18.1 %copy-start.1 = (bf16[8,2,8192]{2,1,0:T(2,128)(2,1)S(1)}, bf16[8,2,8192]{2,1,0:T(2,128)(2,1)}, u32[]{:S(2)}) copy-start(bf16[8,2,8192]{2,1,0:T(2,128)(2,1)} %param.15) | copy-start | bytes 786436
  10.3 23.5 %all-to-all-start.1 = ((s32[32,1,2]{2,1,0:T(1,128)}), s32[32,1,2]{2,1,0:T(1,128)S(1)}, u32[]{:S(2)}, u32[]{:S(2)}) async-start(s32[32,1,2]{2,1,0:T(1,128)} %bitcast.18), calls=%async_computation.1 | async-start | bytes 32768 | tf_op jit(solution)/shard_map/all_to_all | solution.py:184
  23.8 141.0 %all-gather.3.cloned.1.call-start = ((), (), s32[]{:S(2)}) async-start(), calls=%async_computation.4 | async-start | bytes 2228224 | tf_op jit(solution)/shard_map/all_gather | solution.py:140
  33.8 59.1 %all-to-all-start = ((bf16[32,2,2,8192]{3,2,1,0:T(2,128)(2,1)}), bf16[32,2,2,8192]{3,2,1,0:T(2,128)(2,1)S(1)}, u32[]{:S(2)}, u32[]{:S(2)}) async-start(bf16[32,2,2,8192]{3,2,1,0:T(2,128)(2,1)} %broadcast_select_fusion), calls=%async_computation | async-start | bytes 4194304 | tf_op jit(solution)/shard_map/all_to_all | solution.py:183
  43.6 130.4 %all-gather.5.cloned.1.call-start = ((), (), s32[]{:S(2)}) async-start(), calls=%async_computation.5 | async-start | bytes 2228224 | tf_op jit(solution)/shard_map/all_gather | solution.py:141
  44.6 2.8 %copy-start.3 = (bf16[2,256,1024]{2,1,0:T(8,128)(2,1)S(1)}, bf16[2,256,1024]{2,1,0:T(8,128)(2,1)}, u32[]{:S(2)}) copy-start(bf16[2,256,1024]{2,1,0:T(8,128)(2,1)} %param.24) | copy-start | bytes 3145732
  47.4 1.4 copy-start.7
  137.9 8.4 %copy-start.9 = (bf16[8,2,1024]{2,1,0:T(2,128)(2,1)S(1)}, bf16[8,2,1024]{2,1,0:T(2,128)(2,1)}, u32[]{:S(2)}) copy-start(bf16[8,2,1024]{2,1,0:T(2,128)(2,1)} %param.16) | copy-start | bytes 98308
  140.0 14.1 %all-to-all-start.2 = ((f32[32,1,256]{2,1,0:T(1,128)}), f32[32,1,256]{2,1,0:T(1,128)S(1)}, u32[]{:S(2)}, u32[]{:S(2)}) async-start(f32[32,1,256]{2,1,0:T(1,128)} %reshape.535), calls=%async_computation.2 | async-start | bytes 65536 | tf_op jit(solution)/shard_map/all_to_all | solution.py:193
  150.9 10.5 %copy-start.10 = (s32[8]{0:T(128)S(1)}, s32[8]{0:T(128)}, u32[]{:S(2)}) copy-start(s32[8]{0:T(128)} %param.20) | copy-start | bytes 100
  150.9 10.6 %copy-start.8 = (bf16[8,32,1024]{2,1,0:T(8,128)(2,1)S(1)}, bf16[8,32,1024]{2,1,0:T(8,128)(2,1)}, u32[]{:S(2)}) copy-start(bf16[8,32,1024]{2,1,0:T(8,128)(2,1)} %param.18) | copy-start | bytes 1572868
  154.1 0.6 copy-start.4
  154.7 54.5 %all-to-all-start.3 = ((bf16[32,2,2,8192]{3,2,1,0:T(2,128)(2,1)}), bf16[32,2,2,8192]{3,2,1,0:T(2,128)(2,1)}, u32[]{:S(2)}, u32[]{:S(2)}) async-start(bf16[32,2,2,8192]{3,2,1,0:T(2,128)(2,1)} %reshape.489), calls=%async_computation.3 | async-start | bytes 4194304 | tf_op jit(solution)/shard_map/all_to_all | solution.py:190
  161.4 3.0 %copy-start.6 = (bf16[8,2,1024]{2,1,0:T(2,128)(2,1)S(1)}, bf16[8,2,1024]{2,1,0:T(2,128)(2,1)}, u32[]{:S(2)}) copy-start(bf16[8,2,1024]{2,1,0:T(2,128)(2,1)} %param.17) | copy-start | bytes 98308
  164.8 2.9 %copy-start.2 = (bf16[8,8,2,8,128]{4,3,2,1,0:T(8,128)(2,1)S(1)}, bf16[8,8,2,8,128]{4,3,2,1,0:T(8,128)(2,1)}, u32[]{:S(2)}) copy-start(bf16[8,8,2,8,128]{4,3,2,1,0:T(8,128)(2,1)} %copy.114) | copy-start | bytes 786436
  180.4 0.9 copy-start.5
Sparse Core Ops, SparseCore 0:
  26.7 42.4 all-gather.2
  71.3 41.1 all-gather.4
where the time goes:
time: 224 us; the launch traced here: 223 us
  waiting for transfers between devices  72.9 us (33%)
  local copies, waits for them, and re-layouts  47.7 us (21%)
  matrix products  36.3 us (16%)
  starting transfers between devices  36.2 us (16%)
  other arithmetic  15.3 us (7%)
  between operations  13.9 us (6%)
    all_to_all x1, waiting for transfers between devices, shards(): lax.all_to_all(send_queries, 'dev', split_axis=0, concat_axis=0, tiled=True)  43.7 us
    all_to_all x1, waiting for transfers between devices, shards(): lax.all_to_all(answers.astype(jnp.float32), 'dev', split_axis=0, concat_a...  24.5 us
    dot_general x8, matrix products, one_head(): jnp.dot(weights.astype(jnp.bfloat16), head_values, preferred_element_type...  17.1 us
    all_to_all x1, starting transfers between devices, shards(): lax.all_to_all(send_slots, 'dev', split_axis=0, concat_axis=0, tiled=True)  13.4 us
    dot_general x8, matrix products, one_head(): jnp.einsum('qd,ld->ql', head_queries, head_keys, preferred_element_type=j...  12 us
    all_to_all x1, starting transfers between devices, shards(): lax.all_to_all(send_queries, 'dev', split_axis=0, concat_axis=0, tiled=True)  9.78 us
    all_to_all x1, starting transfers between devices, shards(): lax.all_to_all(answers.astype(jnp.float32), 'dev', split_axis=0, concat_a...  6.59 us
    unnamed x29, local copies, waits for them, and re-layouts  6.46 us
  transfers between devices with their start and end apart: 6, of which 3 were waited for; matrix products, arithmetic and copies ran while one was open for 40% of the time, Pallas kernels for 0%

commit v1 on v0

v1 whole, which is shorter than its diff:
```python
import functools
import math

import jax
import jax.numpy as jnp
from jax import lax
from jax.experimental import pallas as pl
from jax.experimental.pallas import tpu as pltpu
from jax.sharding import PartitionSpec as P

KV = 8
HEAD = 128
NX = 4
CORES = 2
REQ = 8
ROWS = 128
SLOT_ROWS = 32
BLK = 256
SUF = 32
LOCAL = 384
HALF = KV // 2
FLOOR = -1.0e30
DROP = -2.0e30
SCALE = 1.0 / math.sqrt(HEAD)
SCALE2 = SCALE / math.log(2.0)
MESH = pl.DeviceIdType.MESH
NT = (((1,), (1,)), ((), ()))


def iota(shape, dim):
    return lax.broadcasted_iota(jnp.int32, shape, dim)


def kernel(
    nz,
    ny,
    q_ref,
    nk_ref,
    nv_ref,
    sk_ref,
    sv_ref,
    rk_ref,
    rv_ref,
    pk_ref,
    pv_ref,
    slen_ref,
    plen_ref,
    om_ref,
    bl_ref,
    out_ref,
    zq,
    snd,
    rcv,
    ans,
    ret,
    rsin,
    rsout,
    rkv,
    pk,
    pv,
    sk,
    sv,
    metaz,
    metax,
    onehot,
    bias_t,
    pick,
    kbias,
    lbias,
    lpick,
    lmine,
    lret,
    lslot,
    lin,
    lout,
    loc_acc,
    loc_max,
    loc_tot,
    lacc,
    local_sem,
    zs_sem,
    zr_sem,
    ms_sem,
    mr_sem,
    nsend_sem,
    nrecv_sem,
    xs_sem,
    xr_sem,
    bs_sem,
    br_sem,
    ls_sem,
    lr_sem,
    rs_sem,
    rr_sem,
    es_sem,
    er_sem,
    ys_sem,
    yr_sem,
    cs_sem,
    cr_sem,
):
    zh = nz // 2
    yh = ny // 2
    group = lax.axis_index("group")
    dev = lax.axis_index("dev")
    z, x = dev // NX, dev % NX
    y, core = group // CORES, group % CORES

    def at_z(step):
        return (group, lax.rem(z + step + nz, nz) * NX + x)

    def at_x(step):
        return (group, z * NX + lax.rem(x + step, NX))

    def at_y(step):
        return (lax.rem(y + step + ny, ny) * CORES + core, dev)

    sibling = (y * CORES + 1 - core, dev)
    drains = []

    def send(src, dst, send_sem, recv_sem, device):
        copy = pltpu.make_async_remote_copy(
            src_ref=src,
            dst_ref=dst,
            send_sem=send_sem,
            recv_sem=recv_sem,
            device_id=device,
            device_id_type=MESH,
        )
        copy.start()
        drains.append(copy)

    def arrived(ref, send_sem, recv_sem, device):
        pltpu.make_async_remote_copy(
            src_ref=ref,
            dst_ref=ref,
            send_sem=send_sem,
            recv_sem=recv_sem,
            device_id=device,
            device_id_type=MESH,
        ).wait_recv()

    loads = [
        pltpu.make_async_copy(rk_ref, rkv.at[0, 0], local_sem.at[0]),
        pltpu.make_async_copy(rv_ref, rkv.at[0, 1], local_sem.at[1]),
        pltpu.make_async_copy(pk_ref, pk, local_sem.at[2]),
        pltpu.make_async_copy(pv_ref, pv, local_sem.at[3]),
        pltpu.make_async_copy(sk_ref, sk.at[pl.ds(0, REQ * SUF)], local_sem.at[4]),
        pltpu.make_async_copy(sv_ref, sv.at[pl.ds(0, REQ * SUF)], local_sem.at[5]),
    ]
    for load in loads:
        load.start()

    partners = [at_z(step) for step in range(1, nz)]
    partners += [at_x(step) for step in range(1, NX)]
    if ny > 1:
        partners += [at_y(1), at_y(-1)]
    partners += [sibling]
    barrier = pltpu.get_barrier_semaphore()
    for partner in partners:
        pl.semaphore_signal(barrier, inc=1, device_id=partner, device_id_type=MESH)

    lane1 = iota((1, ROWS), 1)
    stored = [om_ref[0, bl_ref[p // 2, p % 2]] for p in range(2 * REQ)]
    owner = [s // 2 for s in stored]
    code_rows = [jnp.zeros((1, ROWS), jnp.int32), jnp.zeros((1, ROWS), jnp.int32)]
    for p in range(2 * REQ):
        rank = jnp.int32(0)
        for other in range(p):
            rank = rank + (owner[other] == owner[p]).astype(jnp.int32)
        code = owner[p] * 4 + rank * 2 + stored[p] % 2
        code_rows[p % 2] = jnp.where(lane1 // 16 == p // 2, code, code_rows[p % 2])
    metaz[0, pl.ds(0, 1), :] = code_rows[0]
    metaz[0, pl.ds(1, 1), :] = code_rows[1]

    pl.semaphore_wait(barrier, len(partners))

    def q_half(b, h):
        rows = pl.ds(h * HALF, HALF)
        return q_ref.at[rows] if b == 0 else zq.at[b, rows]

    def pass_queries(b, h, step, into):
        send(
            q_half(b, h),
            zq.at[into, pl.ds(h * HALF, HALF)],
            zs_sem.at[into, h],
            zr_sem.at[into, h],
            at_z(step),
        )

    def forward_queries(b, h):
        for step in (1, -1):
            if b == 0 or (step == 1) == (b > zh):
                if b == zh:
                    continue
                into = (b - step) % nz
                if into == zh and h != (0 if step == 1 else 1):
                    continue
                pass_queries(b, h, step, into)

    def query_arrived(b, h):
        arrived(
            zq.at[b, pl.ds(h * HALF, HALF)], zs_sem.at[b, h], zr_sem.at[b, h], at_z(1)
        )

    for h in range(2):
        forward_queries(0, h)
    for step in range(1, nz):
        send(
            metaz.at[0],
            metaz.at[(-step) % nz],
            ms_sem.at[step],
            mr_sem.at[(-step) % nz],
            at_z(step),
        )

    loads[0].wait()
    loads[1].wait()

    def share_root(b):
        send(rkv.at[b], rkv.at[ny + b], cs_sem.at[b], cr_sem.at[b], sibling)

    def forward_root(b):
        for step in (1, -1):
            if b == 0 or (step == 1) == (b > yh):
                if b == yh or ny == 1:
                    continue
                into = (b - step) % ny
                if into == yh:
                    part = 0 if step == 1 else 1
                    send(
                        rkv.at[b, part],
                        rkv.at[into, part],
                        ys_sem.at[into, part],
                        yr_sem.at[into, part],
                        at_y(step),
                    )
                else:
                    send(
                        rkv.at[b],
                        rkv.at[into],
                        ys_sem.at[into, 0],
                        yr_sem.at[into, 0],
                        at_y(step),
                    )

    def root_arrived(b):
        if b == yh:
            for part in range(2):
                arrived(rkv.at[b, part], ys_sem.at[b, part], yr_sem.at[b, part], at_y(1))
        else:
            arrived(rkv.at[b], ys_sem.at[b, 0], yr_sem.at[b, 0], at_y(1))

    forward_root(0)
    share_root(0)

    row = iota((ROWS, ROWS), 0)
    lane = iota((ROWS, ROWS), 1)
    same_place = row % 16 == lane % 16
    diagonal = jnp.where(row == lane, 0.0, DROP)

    def select(b):
        wanted = z * (2 * NX) + row // 16
        first = metaz[b, pl.ds(0, 1), :] // 2
        second = metaz[b, pl.ds(1, 1), :] // 2
        hit = ((first == wanted) | (second == wanted)) & same_place
        onehot[b] = jnp.where(hit, 1.0, 0.0).astype(jnp.bfloat16)
        bias_t[b] = jnp.where(hit, 0.0, DROP).T
        mine = pl.ds(pl.multiple_of(x * SLOT_ROWS, SLOT_ROWS), SLOT_ROWS)

        def body(k, carry):
            block = q_ref[k] if b == 0 else zq[b, k]
            chosen = jnp.dot(onehot[b], block, preferred_element_type=jnp.float32)
            snd[b, k] = chosen.astype(jnp.bfloat16)
            rcv[b, k, mine, :] = snd[b, k, mine, :]
            return carry

        lax.fori_loop(0, KV, body, 0)
        for step in range(1, NX):
            there = pl.ds(pl.multiple_of(lax.rem(x + step, NX) * SLOT_ROWS, SLOT_ROWS), SLOT_ROWS)
            send(
                snd.at[b, :, there, :],
                rcv.at[b, :, mine, :],
                xs_sem.at[b, NX - step],
                xr_sem.at[b, NX - step],
                at_x(step),
            )

    def slots_arrived(b):
        for step in range(1, NX):
            there = pl.ds(pl.multiple_of(lax.rem(x + step, NX) * SLOT_ROWS, SLOT_ROWS), SLOT_ROWS)
            arrived(
                rcv.at[b, :, there, :], xs_sem.at[b, step], xr_sem.at[b, step], at_x(step)
            )

    ones_prefix = jnp.ones((2 * BLK, HEAD), jnp.bfloat16)

    def serve(b):
        slots_arrived(b)
        for source in range(NX):
            code = metax[source, b]
            srow = iota((SLOT_ROWS, ROWS), 0)
            slane = iota((SLOT_ROWS, ROWS), 1)
            wanted = (dev * 2 + srow // 16) * 2 + 1
            hit = (code[0:1, :] == wanted) | (code[1:2, :] == wanted)
            second = jnp.max(jnp.where(hit, 1.0, 0.0), axis=1, keepdims=True)
            pick[b, pl.ds(source * SLOT_ROWS, SLOT_ROWS), :] = jnp.where(
                slane == 0, 1.0 - second, jnp.where(slane == 1, second, 0.0)
            ).astype(jnp.bfloat16)

        def body(k, carry):
            cols = pl.ds(pl.multiple_of(k * HEAD, HEAD), HEAD)
            queries = jnp.concatenate([rcv[b, k], pick[b]], axis=1)
            keys = jnp.concatenate([pk[:, cols], kbias[...]], axis=1)
            scores = lax.dot_general(queries, keys, NT, preferred_element_type=jnp.float32)
            highest = jnp.max(scores, axis=1, keepdims=True)
            weights = jnp.exp2((scores - highest) * SCALE2).astype(jnp.bfloat16)
            values = jnp.concatenate([pv[:, cols], ones_prefix], axis=1)
            summed = jnp.dot(weights, values, preferred_element_type=jnp.float32)
            totals = summed[:, HEAD:]
            ans[b, k] = (summed[:, :HEAD] / totals).astype(jnp.bfloat16)
            lacc[...] = jnp.where(lane == k, highest * SCALE + jnp.log(totals), lacc[...])
            return carry

        lax.fori_loop(0, KV, body, 0)
        lmine[b] = lacc[...].T[:KV, :]

    def give_back(b):
        mine = pl.ds(pl.multiple_of(x * SLOT_ROWS, SLOT_ROWS), SLOT_ROWS)
        for step in range(1, NX):
            there = pl.ds(pl.multiple_of(lax.rem(x + step, NX) * SLOT_ROWS, SLOT_ROWS), SLOT_ROWS)
            send(
                ans.at[b, :, there, :],
                ret.at[b, :, mine, :],
                bs_sem.at[b, NX - step],
                br_sem.at[b, NX - step],
                at_x(step),
            )
            send(
                lmine.at[b],
                lret.at[b, NX - step],
                ls_sem.at[b, NX - step],
                lr_sem.at[b, NX - step],
                at_x(step),
            )

        def body(k, carry):
            ret[b, k, mine, :] = ans[b, k, mine, :]
            return carry

        lax.fori_loop(0, KV, body, 0)

    def answers_arrived(b):
        lane8 = iota((KV, ROWS), 1)
        rows = lmine[b]
        for step in range(1, NX):
            there = pl.ds(pl.multiple_of(lax.rem(x + step, NX) * SLOT_ROWS, SLOT_ROWS), SLOT_ROWS)
            arrived(
                ret.at[b, :, there, :], bs_sem.at[b, step], br_sem.at[b, step], at_x(step)
            )
            arrived(lret.at[b, step], ls_sem.at[b, step], lr_sem.at[b, step], at_x(step))
            moved = pltpu.roll(lret[b, step], SLOT_ROWS * step, 1)
            rows = jnp.where(lane8 // SLOT_ROWS == lax.rem(x + step, NX), moved, rows)
        lslot[b] = rows

    def chain(b, h):
        step = 1 if b < zh or (b == zh and h == 0) else -1
        into = (b - step) % nz
        place = into if into else (0 if step == 1 else zh)
        return step, place

    def has_input(b, h):
        return b != zh and (b not in (zh - 1, zh + 1) or chain(zh, h)[1] == b)

    def partial_arrived(place, h):
        arrived(
            rsin.at[place, pl.ds(h * HALF, HALF)],
            rs_sem.at[place, h],
            rr_sem.at[place, h],
            at_z(1),
        )
        arrived(lin.at[place, h], es_sem.at[place, h], er_sem.at[place, h], at_z(1))

    def combine(b, h):
        fed = has_input(b, h)
        if fed:
            partial_arrived(b, h)

        def body(k, carry):
            rows = jnp.broadcast_to(lslot[b, pl.ds(k, 1), :], (ROWS, ROWS)) + bias_t[b]
            parts = ret[b, k]
            if fed:
                extra = jnp.broadcast_to(lin[b, h, pl.ds(k, 1), :], (ROWS, ROWS)) + diagonal
                rows = jnp.concatenate([rows, extra], axis=1)
                parts = jnp.concatenate([parts, rsin[b, k]], axis=0)
            highest = jnp.maximum(jnp.max(rows, axis=1, keepdims=True), FLOOR)
            weights = jnp.exp(rows - highest).astype(jnp.bfloat16)
            parts = jnp.concatenate([parts, jnp.ones_like(parts)], axis=1)
            summed = jnp.dot(weights, parts, preferred_element_type=jnp.float32)
            totals = jnp.maximum(summed[:, HEAD:], 1.0e-30)
            rsout[b, k] = (summed[:, :HEAD] / totals).astype(jnp.bfloat16)
            lacc[...] = jnp.where(lane == k, highest + jnp.log(totals), lacc[...])
            return carry

        lax.fori_loop(h * HALF, (h + 1) * HALF, body, 0)
        lout[b, h] = lacc[...].T[:KV, :]
        step, place = chain(b, h)
        part = pl.ds(h * HALF, HALF)
        send(
            rsout.at[b, part],
            rsin.at[place, part],
            rs_sem.at[place, h],
            rr_sem.at[place, h],
            at_z(step),
        )
        send(
            lout.at[b, h],
            lin.at[place, h],
            es_sem.at[place, h],
            er_sem.at[place, h],
            at_z(step),
        )

    ones_root = jnp.ones((ny * CORES * rkv.shape[2], HEAD), jnp.bfloat16)
    ones_local = jnp.ones((LOCAL, HEAD), jnp.bfloat16)
    root_rows = ny * CORES * rkv.shape[2]

    def attend_local(k_from, k_to):
        def body(k, carry):
            cols = pl.ds(pl.multiple_of(k * HEAD, HEAD), HEAD)
            queries = q_ref[k]
            root_keys = rkv[:, 0, :, cols].reshape(root_rows, HEAD)
            root_values = rkv[:, 1, :, cols].reshape(root_rows, HEAD)
            root_scores = lax.dot_general(
                queries, root_keys, NT, preferred_element_type=jnp.float32
            )
            wide = jnp.concatenate([queries, lpick[...]], axis=1)
            keys = jnp.concatenate([sk[:, cols], lbias[...]], axis=1)
            scores = lax.dot_general(wide, keys, NT, preferred_element_type=jnp.float32)
            highest = jnp.maximum(
                jnp.max(root_scores, axis=1, keepdims=True),
                jnp.max(scores, axis=1, keepdims=True),
            )
            root_weights = jnp.exp2((root_scores - highest) * SCALE2).astype(jnp.bfloat16)
            weights = jnp.exp2((scores - highest) * SCALE2).astype(jnp.bfloat16)
            summed = jnp.dot(
                root_weights,
                jnp.concatenate([root_values, ones_root], axis=1),
                preferred_element_type=jnp.float32,
            ) + jnp.dot(
                weights,
                jnp.concatenate([sv[:, cols], ones_local], axis=1),
                preferred_element_type=jnp.float32,
            )
            loc_acc[k] = summed[:, :HEAD]
            loc_tot[k] = summed[:, HEAD:]
            loc_max[k] = jnp.broadcast_to(highest * SCALE, (ROWS, ROWS))
            return carry

        lax.fori_loop(k_from, k_to, body, 0)

    def finish(h):
        partial_arrived(0, h)
        partial_arrived(zh, h)

        def body(k, carry):
            rows = jnp.concatenate(
                [
                    jnp.broadcast_to(lslot[0, pl.ds(k, 1), :], (ROWS, ROWS)) + bias_t[0],
                    jnp.broadcast_to(lin[0, h, pl.ds(k, 1), :], (ROWS, ROWS)) + diagonal,
                    jnp.broadcast_to(lin[zh, h, pl.ds(k, 1), :], (ROWS, ROWS)) + diagonal,
                ],
                axis=1,
            )
            highest = jnp.maximum(jnp.max(rows, axis=1, keepdims=True), loc_max[k])
            wide = jnp.concatenate([highest] * 3, axis=1)
            weights = jnp.exp(rows - wide).astype(jnp.bfloat16)
            parts = jnp.concatenate([ret[0, k], rsin[0, k], rsin[zh, k]], axis=0)
            parts = jnp.concatenate([parts, jnp.ones_like(parts)], axis=1)
            summed = jnp.dot(weights, parts, preferred_element_type=jnp.float32)
            share = jnp.exp(loc_max[k] - highest)
            numerator = summed[:, :HEAD] + loc_acc[k] * share
            denominator = summed[:, HEAD:] + loc_tot[k] * share
            out_ref[k] = (numerator / denominator).astype(jnp.bfloat16)
            return carry

        lax.fori_loop(h * HALF, (h + 1) * HALF, body, 0)

    lacc[...] = jnp.zeros_like(lacc)
    select(0)

    for b in range(1, nz):
        arrived(metaz.at[b], ms_sem.at[b], mr_sem.at[b], at_z(1))
    for step in range(1, NX):
        send(
            metaz,
            metax.at[x],
            nsend_sem.at[NX - step],
            nrecv_sem.at[NX - step],
            at_x(step),
        )
    metax[x] = metaz[...]

    prow = iota((2 * BLK, HEAD), 0)
    plane = iota((2 * BLK, HEAD), 1)
    limit = jnp.where(prow < BLK, plen_ref[0], plen_ref[1])
    live = prow % BLK < limit
    kbias[...] = jnp.where(
        (plane < 2) & ~((plane == prow // BLK) & live), DROP, 0.0
    ).astype(jnp.bfloat16)
    lrow = iota((LOCAL, HEAD), 0)
    llane = iota((LOCAL, HEAD), 1)
    length = jnp.zeros((LOCAL, HEAD), jnp.int32)
    for r in range(REQ):
        length = jnp.where(lrow // SUF == r, slen_ref[r], length)
    past = (lrow < REQ * SUF) & (llane // 2 == lrow // SUF) & (lrow % SUF < length)
    fresh_row = lrow - REQ * SUF
    fresh = (
        (fresh_row >= 0)
        & (fresh_row < 2 * REQ)
        & (llane // 2 == fresh_row // 2)
        & (fresh_row % 2 <= llane % 2)
    )
    lbias[...] = jnp.where((llane < 2 * REQ) & ~(past | fresh), DROP, 0.0).astype(jnp.bfloat16)
    lpick[...] = jnp.where(lane == row // 8, 1.0, 0.0).astype(jnp.bfloat16)
    blank = jnp.zeros((LOCAL - REQ * SUF - 2 * REQ, KV * HEAD), jnp.bfloat16)
    for cache, new in ((sk, nk_ref), (sv, nv_ref)):
        cache[pl.ds(REQ * SUF, 2 * REQ), :] = new[...]
        cache[pl.ds(REQ * SUF + 2 * REQ, LOCAL - REQ * SUF - 2 * REQ), :] = blank

    for load in loads[2:]:
        load.wait()
    meta_waited = False

    waiting = [0]
    for s in range(1, zh + 1):
        blocks = (nz - s, s) if s < zh else (zh,)
        for h in range(2):
            for b in blocks:
                query_arrived(b, h)
                forward_queries(b, h)
        for b in blocks:
            select(b)
        if s <= yh:
            for b in (ny - s, s) if s < yh else (yh,):
                root_arrived(b)
                forward_root(b)
                share_root(b)
        if not meta_waited:
            meta_waited = True
            for step in range(1, NX):
                arrived(
                    metax.at[lax.rem(x + step, NX)],
                    nsend_sem.at[step],
                    nrecv_sem.at[step],
                    at_x(step),
                )
        for b in waiting:
            serve(b)
        waiting = list(blocks)
    for s in range(zh + 1, yh + 1):
        for b in (ny - s, s) if s < yh else (yh,):
            root_arrived(b)
            forward_root(b)
            share_root(b)

    for b in waiting:
        serve(b)
    give_back(zh)
    order = [(zh,)] + [(s, nz - s) for s in range(zh - 1, 0, -1)] + [(0,)]
    for b in order[1]:
        give_back(b)

    for b in range(ny):
        arrived(rkv.at[ny + b], cs_sem.at[b], cr_sem.at[b], sibling)
    per_turn = -(-KV // zh)
    done = 0
    for turn, blocks in enumerate(order[:-1]):
        for b in blocks:
            answers_arrived(b)
        for h in range(2):
            for b in blocks:
                combine(b, h)
        if turn + 2 < len(order):
            for b in order[turn + 2]:
                give_back(b)
        upto = min(KV, done + per_turn)
        if done < upto:
            attend_local(done, upto)
        done = upto
    answers_arrived(0)
    for h in range(2):
        finish(h)

    for copy in drains:
        copy.wait_send()


def shards(nz, ny, *args):
    (
        queries,
        new_keys,
        new_values,
        suffix_keys,
        suffix_values,
        suffix_lengths,
        root_keys,
        root_values,
        prefix_keys,
        prefix_values,
        prefix_lengths,
        owner_map,
        block_lists,
    ) = args
    width = KV * HEAD
    head_major = (
        queries.reshape(REQ, 2, KV, 8, HEAD).transpose(2, 0, 1, 3, 4).reshape(KV, ROWS, HEAD)
    )
    root_rows = root_keys.shape[0]
    bf16, f32 = jnp.bfloat16, jnp.float32
    vmem = pl.BlockSpec(memory_space=pltpu.VMEM)
    smem = pl.BlockSpec(memory_space=pltpu.SMEM)
    anywhere = pl.BlockSpec(memory_space=pl.ANY)
    dma = pltpu.SemaphoreType.DMA
    blocks = (nz, KV, ROWS, HEAD)
    out = pl.pallas_call(
        functools.partial(kernel, nz, ny),
        out_shape=jax.ShapeDtypeStruct((KV, ROWS, HEAD), bf16),
        in_specs=[vmem, vmem, vmem] + [anywhere] * 6 + [smem] * 4,
        out_specs=vmem,
        scratch_shapes=[
            pltpu.VMEM(blocks, bf16),
            pltpu.VMEM(blocks, bf16),
            pltpu.VMEM(blocks, bf16),
            pltpu.VMEM(blocks, bf16),
            pltpu.VMEM(blocks, bf16),
            pltpu.VMEM(blocks, bf16),
            pltpu.VMEM(blocks, bf16),
            pltpu.VMEM((2 * ny, 2, root_rows, width), bf16),
            pltpu.VMEM((2 * BLK, width), bf16),
            pltpu.VMEM((2 * BLK, width), bf16),
            pltpu.VMEM((LOCAL, width), bf16),
            pltpu.VMEM((LOCAL, width), bf16),
            pltpu.VMEM((nz, 2, ROWS), jnp.int32),
            pltpu.VMEM((NX, nz, 2, ROWS), jnp.int32),
            pltpu.VMEM((nz, ROWS, ROWS), bf16),
            pltpu.VMEM((nz, ROWS, ROWS), f32),
            pltpu.VMEM((nz, ROWS, HEAD), bf16),
            pltpu.VMEM((2 * BLK, HEAD), bf16),
            pltpu.VMEM((LOCAL, HEAD), bf16),
            pltpu.VMEM((ROWS, HEAD), bf16),
            pltpu.VMEM((nz, KV, ROWS), f32),
            pltpu.VMEM((nz, NX, KV, ROWS), f32),
            pltpu.VMEM((nz, KV, ROWS), f32),
            pltpu.VMEM((nz, 2, KV, ROWS), f32),
            pltpu.VMEM((nz, 2, KV, ROWS), f32),
            pltpu.VMEM((KV, ROWS, HEAD), f32),
            pltpu.VMEM((KV, ROWS, HEAD), f32),
            pltpu.VMEM((KV, ROWS, HEAD), f32),
            pltpu.VMEM((ROWS, ROWS), f32),
            dma((6,)),
            dma((nz, 2)),
            dma((nz, 2)),
            dma((nz,)),
            dma((nz,)),
            dma((NX,)),
            dma((NX,)),
            dma((nz, NX)),
            dma((nz, NX)),
            dma((nz, NX)),
            dma((nz, NX)),
            dma((nz, NX)),
            dma((nz, NX)),
            dma((nz, 2)),
            dma((nz, 2)),
            dma((nz, 2)),
            dma((nz, 2)),
            dma((ny, 2)),
            dma((ny, 2)),
            dma((ny,)),
            dma((ny,)),
        ],
        compiler_params=pltpu.CompilerParams(
            collective_id=0, has_side_effects=True, vmem_limit_bytes=48 * 1024 * 1024
        ),
        cost_estimate=pl.CostEstimate(
            flops=4_000_000_000, bytes_accessed=5_000_000, transcendentals=8_000_000
        ),
        name="shared_prefix_attention",
    )(
        head_major,
        new_keys.reshape(2 * REQ, width),
        new_values.reshape(2 * REQ, width),
        suffix_keys.reshape(REQ * SUF, width),
        suffix_values.reshape(REQ * SUF, width),
        root_keys,
        root_values,
        prefix_keys.reshape(2 * BLK, width),
        prefix_values.reshape(2 * BLK, width),
        suffix_lengths,
        prefix_lengths,
        owner_map,
        block_lists,
    )
    return out.reshape(KV, REQ, 2, 8, HEAD).transpose(1, 2, 0, 3, 4).reshape(REQ, 2, 64 * HEAD)


def solution(mesh):
    return jax.shard_map(
        functools.partial(shards, mesh.shape["dev"] // NX, mesh.shape["group"] // CORES),
        mesh=mesh,
        in_specs=(
            P(("group", "dev"), None, None),
            P(("group", "dev"), None, None),
            P(("group", "dev"), None, None),
            P(("group", "dev"), None, None),
            P(("group", "dev"), None, None),
            P(("group", "dev")),
            P("group", None),
            P("group", None),
            P(("group", "dev"), None, None),
            P(("group", "dev"), None, None),
            P(("group", "dev")),
            P("group", None),
            P(("group", "dev"), None),
        ),
        out_specs=P(("group", "dev"), None, None),
        check_vma=False,
    )
```

time: 224 us -> 113 us (0.50)
  the two profiles are of different devices: /device:TPU:12 before, /device:TPU:24 now
where the time goes in v1:
time: 113 us; the launch traced here: 112 us
  Pallas kernels  103 us (91%)
  local copies, waits for them, and re-layouts  9.46 us (8%)
    pallas_call x1, Pallas kernels, shards(): pl.pallas_call(functools.partial(kernel, nz, ny), out_shape=jax.ShapeDtyp...  103 us
    unnamed x19, local copies, waits for them, and re-layouts  5.87 us

profile of v1, /device:TPU:24, one launch (start us, length us, event | category | flops | bytes accessed | tf_op | source)
XLA Modules:
  0.0 112.4 jit_solution(16776869546129718080)
XLA Ops:
  0.0 0.0 copy-start
  0.0 0.8 copy.15.bl_ref
  0.8 0.8 reshape.32.nk_ref
  1.6 0.8 reshape.33.nv_ref
  2.4 1.2 %reshape.30 = bf16[8,2,8,8,128]{4,3,2,1,0:T(8,128)(2,1)S(1)} reshape(bf16[8,2,8192]{2,1,0:T(2,128)(2,1)} %param.13) | data formatting | bytes 524288 | tf_op jit(solution)/shard_map/reshape | solution.py:617
  3.6 0.0 copy-start.4
  3.6 0.0 copy-start.6
  3.6 0.0 copy-start.7
  3.7 0.0 copy-start.8
  3.7 0.0 copy-done
  3.7 0.8 copy-done.4
  4.5 0.0 copy-done.6
  4.5 0.0 copy-done.7
  4.5 0.0 copy-done.8
  4.5 0.0 copy-start.1
  4.5 1.2 %copy-done.1 = bf16[2,256,1024]{2,1,0:T(8,128)(2,1)S(1)} copy-done((bf16[2,256,1024]{2,1,0:T(8,128)(2,1)S(1)}, bf16[2,256,1024]{2,1,0:T(8,128)(2,1)}, u32[]{:S(2)}) %copy-start.1) | copy-done | bytes 1048600
  5.7 0.0 copy-start.2
  5.7 1.0 copy-done.2
  6.7 0.0 copy-start.3
  6.7 1.0 copy-done.3
  7.8 0.9 copy-done.5
  8.7 102.9 %shared_prefix_attention.1 = bf16[8,128,128]{2,1,0:T(8,128)(2,1)S(1)} custom-call(bf16[8,128,128]{2,1,0:T(8,128)(2,1)S(1)} %bitcast.12, bf16[16,1024]{1,0:T(8,128)(2,1)S(1)} %reshape.32.nk_ref, bf16[16,1024]{1,0:T(8,128)(2,1)S(1)} %reshape.33.nv_ref, bf16[256,1024]{1,0:T(8,128)(2,1)S(1)} %bitcast.16, bf16[256,1024]{1,0:T(8,128)(2,1)S(1)} %bitcast.17, ...), custom_call_target="tpu_custom_call" | custom-call | flops 4000000000 | bytes 5000000 | tf_op jit(solution)/shard_map/shared_prefix_attention/pallas_call | solution.py:626
  111.6 0.1 copy.16
  111.7 0.8 reshape.39
  (2 shorter events, 0.0 us)
Async XLA Ops:
  0.0 3.7 %copy-start = (bf16[2,256,1024]{2,1,0:T(8,128)(2,1)S(1)}, bf16[2,256,1024]{2,1,0:T(8,128)(2,1)}, u32[]{:S(2)}) copy-start(bf16[2,256,1024]{2,1,0:T(8,128)(2,1)} %param.21) | copy-start | bytes 3145732
  3.6 0.9 copy-start.4
  3.6 0.8 copy-start.6
  3.6 0.8 copy-start.7
  3.7 0.8 copy-start.8
  4.5 1.2 %copy-start.1 = (bf16[2,256,1024]{2,1,0:T(8,128)(2,1)S(1)}, bf16[2,256,1024]{2,1,0:T(8,128)(2,1)}, u32[]{:S(2)}) copy-start(bf16[2,256,1024]{2,1,0:T(8,128)(2,1)} %param.22) | copy-start | bytes 3145732
  5.7 1.0 copy-start.2
  6.7 1.0 copy-start.3
  7.8 0.9 copy-start.5

commit v2 on v1

--- a/solution.py
+++ b/solution.py
@@ -22,7 +22,8 @@
 FLOOR = -1.0e30
 DROP = -2.0e30
 SCALE = 1.0 / math.sqrt(HEAD)
-SCALE2 = SCALE / math.log(2.0)
+LOG2E = 1.0 / math.log(2.0)
+SCALE2 = SCALE * LOG2E
 MESH = pl.DeviceIdType.MESH
 NT = (((1,), (1,)), ((), ()))
 
@@ -77,6 +78,7 @@
     loc_max,
     loc_tot,
     lacc,
+    second_slot,
     local_sem,
     zs_sem,
     zr_sem,
@@ -161,7 +163,7 @@
         pl.semaphore_signal(barrier, inc=1, device_id=partner, device_id_type=MESH)
 
     lane1 = iota((1, ROWS), 1)
-    stored = [om_ref[0, bl_ref[p // 2, p % 2]] for p in range(2 * REQ)]
+    stored = [om_ref[0, bl_ref[p % 2, p // 2]] for p in range(2 * REQ)]
     owner = [s // 2 for s in stored]
     code_rows = [jnp.zeros((1, ROWS), jnp.int32), jnp.zeros((1, ROWS), jnp.int32)]
     for p in range(2 * REQ):
@@ -272,10 +274,15 @@
             block = q_ref[k] if b == 0 else zq[b, k]
             chosen = jnp.dot(onehot[b], block, preferred_element_type=jnp.float32)
             snd[b, k] = chosen.astype(jnp.bfloat16)
+            return carry
+
+        lax.fori_loop(0, KV, body, 0, unroll=4)
+
+        def keep(k, carry):
             rcv[b, k, mine, :] = snd[b, k, mine, :]
             return carry
 
-        lax.fori_loop(0, KV, body, 0)
+        lax.fori_loop(0, KV, keep, 0, unroll=True)
         for step in range(1, NX):
             there = pl.ds(pl.multiple_of(lax.rem(x + step, NX) * SLOT_ROWS, SLOT_ROWS), SLOT_ROWS)
             send(
@@ -293,37 +300,51 @@
                 rcv.at[b, :, there, :], xs_sem.at[b, step], xr_sem.at[b, step], at_x(step)
             )
 
-    ones_prefix = jnp.ones((2 * BLK, HEAD), jnp.bfloat16)
-
-    def serve(b):
-        slots_arrived(b)
-        for source in range(NX):
-            code = metax[source, b]
-            srow = iota((SLOT_ROWS, ROWS), 0)
-            slane = iota((SLOT_ROWS, ROWS), 1)
-            wanted = (dev * 2 + srow // 16) * 2 + 1
-            hit = (code[0:1, :] == wanted) | (code[1:2, :] == wanted)
-            second = jnp.max(jnp.where(hit, 1.0, 0.0), axis=1, keepdims=True)
-            pick[b, pl.ds(source * SLOT_ROWS, SLOT_ROWS), :] = jnp.where(
-                slane == 0, 1.0 - second, jnp.where(slane == 1, second, 0.0)
-            ).astype(jnp.bfloat16)
+    ones_prefix = jnp.ones((BLK, HEAD), jnp.bfloat16)
+
+    def serve(blocks):
+        for b in blocks:
+            slots_arrived(b)
+            for source in range(NX):
+                code = metax[source, b]
+                srow = iota((SLOT_ROWS, ROWS), 0)
+                slane = iota((SLOT_ROWS, ROWS), 1)
+                wanted = (dev * 2 + srow // 16) * 2 + 1
+                hit = (code[0:1, :] == wanted) | (code[1:2, :] == wanted)
+                second = jnp.max(jnp.where(hit, 1.0, 0.0), axis=1, keepdims=True)
+                here = pl.ds(source * SLOT_ROWS, SLOT_ROWS)
+                pick[b, here, :] = jnp.where(
+                    slane == 0, 1.0 - second, jnp.where(slane == 1, second, 0.0)
+                ).astype(jnp.bfloat16)
+                second_slot[b, here, :] = jnp.broadcast_to(second, (SLOT_ROWS, ROWS))
 
         def body(k, carry):
             cols = pl.ds(pl.multiple_of(k * HEAD, HEAD), HEAD)
-            queries = jnp.concatenate([rcv[b, k], pick[b]], axis=1)
+            queries = jnp.concatenate(
+                [jnp.concatenate([rcv[b, k], pick[b]], axis=1) for b in blocks], axis=0
+            )
             keys = jnp.concatenate([pk[:, cols], kbias[...]], axis=1)
-            scores = lax.dot_general(queries, keys, NT, preferred_element_type=jnp.float32)
+            both = lax.dot_general(queries, keys, NT, preferred_element_type=jnp.float32)
+            scores = jnp.maximum(both[:, :BLK], both[:, BLK:])
             highest = jnp.max(scores, axis=1, keepdims=True)
             weights = jnp.exp2((scores - highest) * SCALE2).astype(jnp.bfloat16)
-            values = jnp.concatenate([pv[:, cols], ones_prefix], axis=1)
+            values = jnp.concatenate([pv[:BLK, cols], pv[BLK:, cols], ones_prefix], axis=1)
             summed = jnp.dot(weights, values, preferred_element_type=jnp.float32)
-            totals = summed[:, HEAD:]
-            ans[b, k] = (summed[:, :HEAD] / totals).astype(jnp.bfloat16)
-            lacc[...] = jnp.where(lane == k, highest * SCALE + jnp.log(totals), lacc[...])
+            totals = summed[:, 2 * HEAD :]
+            inverse = 1.0 / totals
+            logs = highest * SCALE2 + jnp.log(totals) * LOG2E
+            for at, b in enumerate(blocks):
+                part = slice(at * ROWS, (at + 1) * ROWS)
+                chosen = jnp.where(
+                    second_slot[b] > 0.5, summed[part, HEAD : 2 * HEAD], summed[part, :HEAD]
+                )
+                ans[b, k] = (chosen * inverse[part]).astype(jnp.bfloat16)
+                lacc[at] = jnp.where(lane == k, logs[part], lacc[at])
             return carry
 
-        lax.fori_loop(0, KV, body, 0)
-        lmine[b] = lacc[...].T[:KV, :]
+        lax.fori_loop(0, KV, body, 0, unroll=2)
+        for at, b in enumerate(blocks):
+            lmine[b] = lacc[at].T[:KV, :]
 
     def give_back(b):
         mine = pl.ds(pl.multiple_of(x * SLOT_ROWS, SLOT_ROWS), SLOT_ROWS)
@@ -348,7 +369,7 @@
             ret[b, k, mine, :] = ans[b, k, mine, :]
             return carry
 
-        lax.fori_loop(0, KV, body, 0)
+        lax.fori_loop(0, KV, body, 0, unroll=True)
 
     def answers_arrived(b):
         lane8 = iota((KV, ROWS), 1)
@@ -381,45 +402,47 @@
         )
         arrived(lin.at[place, h], es_sem.at[place, h], er_sem.at[place, h], at_z(1))
 
-    def combine(b, h):
-        fed = has_input(b, h)
-        if fed:
-            partial_arrived(b, h)
+    def combine(blocks, h):
+        for b in blocks:
+            if has_input(b, h):
+                partial_arrived(b, h)
 
         def body(k, carry):
-            rows = jnp.broadcast_to(lslot[b, pl.ds(k, 1), :], (ROWS, ROWS)) + bias_t[b]
-            parts = ret[b, k]
-            if fed:
-                extra = jnp.broadcast_to(lin[b, h, pl.ds(k, 1), :], (ROWS, ROWS)) + diagonal
-                rows = jnp.concatenate([rows, extra], axis=1)
-                parts = jnp.concatenate([parts, rsin[b, k]], axis=0)
-            highest = jnp.maximum(jnp.max(rows, axis=1, keepdims=True), FLOOR)
-            weights = jnp.exp(rows - highest).astype(jnp.bfloat16)
-            parts = jnp.concatenate([parts, jnp.ones_like(parts)], axis=1)
-            summed = jnp.dot(weights, parts, preferred_element_type=jnp.float32)
-            totals = jnp.maximum(summed[:, HEAD:], 1.0e-30)
-            rsout[b, k] = (summed[:, :HEAD] / totals).astype(jnp.bfloat16)
-            lacc[...] = jnp.where(lane == k, highest + jnp.log(totals), lacc[...])
+            for at, b in enumerate(blocks):
+                rows = jnp.broadcast_to(lslot[b, pl.ds(k, 1), :], (ROWS, ROWS)) + bias_t[b]
+                parts = ret[b, k]
+                if has_input(b, h):
+                    extra = jnp.broadcast_to(lin[b, h, pl.ds(k, 1), :], (ROWS, ROWS)) + diagonal
+                    rows = jnp.concatenate([rows, extra], axis=1)
+                    parts = jnp.concatenate([parts, rsin[b, k]], axis=0)
+                highest = jnp.maximum(jnp.max(rows, axis=1, keepdims=True), FLOOR)
+                weights = jnp.exp2(rows - highest).astype(jnp.bfloat16)
+                parts = jnp.concatenate([parts, jnp.ones_like(parts)], axis=1)
+                summed = jnp.dot(weights, parts, preferred_element_type=jnp.float32)
+                totals = jnp.maximum(summed[:, HEAD:], 1.0e-30)
+                rsout[b, k] = (summed[:, :HEAD] / totals).astype(jnp.bfloat16)
+                lacc[at] = jnp.where(lane == k, highest + jnp.log(totals) * LOG2E, lacc[at])
             return carry
 
-        lax.fori_loop(h * HALF, (h + 1) * HALF, body, 0)
-        lout[b, h] = lacc[...].T[:KV, :]
-        step, place = chain(b, h)
-        part = pl.ds(h * HALF, HALF)
-        send(
-            rsout.at[b, part],
-            rsin.at[place, part],
-            rs_sem.at[place, h],
-            rr_sem.at[place, h],
-            at_z(step),
-        )
-        send(
-            lout.at[b, h],
-            lin.at[place, h],
-            es_sem.at[place, h],
-            er_sem.at[place, h],
-            at_z(step),
-        )
+        lax.fori_loop(h * HALF, (h + 1) * HALF, body, 0, unroll=2)
+        for at, b in enumerate(blocks):
+            lout[b, h] = lacc[at].T[:KV, :]
+            step, place = chain(b, h)
+            part = pl.ds(h * HALF, HALF)
+            send(
+                rsout.at[b, part],
+                rsin.at[place, part],
+                rs_sem.at[place, h],
+                rr_sem.at[place, h],
+                at_z(step),
+            )
+            send(
+                lout.at[b, h],
+                lin.at[place, h],
+                es_sem.at[place, h],
+                er_sem.at[place, h],
+                at_z(step),
+            )
 
     ones_root = jnp.ones((ny * CORES * rkv.shape[2], HEAD), jnp.bfloat16)
     ones_local = jnp.ones((LOCAL, HEAD), jnp.bfloat16)
@@ -454,7 +477,7 @@
             )
             loc_acc[k] = summed[:, :HEAD]
             loc_tot[k] = summed[:, HEAD:]
-            loc_max[k] = jnp.broadcast_to(highest * SCALE, (ROWS, ROWS))
+            loc_max[k] = jnp.broadcast_to(highest * SCALE2, (ROWS, ROWS))
             return carry
 
         lax.fori_loop(k_from, k_to, body, 0)
@@ -474,17 +497,17 @@
             )
             highest = jnp.maximum(jnp.max(rows, axis=1, keepdims=True), loc_max[k])
             wide = jnp.concatenate([highest] * 3, axis=1)
-            weights = jnp.exp(rows - wide).astype(jnp.bfloat16)
+            weights = jnp.exp2(rows - wide).astype(jnp.bfloat16)
             parts = jnp.concatenate([ret[0, k], rsin[0, k], rsin[zh, k]], axis=0)
             parts = jnp.concatenate([parts, jnp.ones_like(parts)], axis=1)
             summed = jnp.dot(weights, parts, preferred_element_type=jnp.float32)
-            share = jnp.exp(loc_max[k] - highest)
+            share = jnp.exp2(loc_max[k] - highest)
             numerator = summed[:, :HEAD] + loc_acc[k] * share
             denominator = summed[:, HEAD:] + loc_tot[k] * share
             out_ref[k] = (numerator / denominator).astype(jnp.bfloat16)
             return carry
 
-        lax.fori_loop(h * HALF, (h + 1) * HALF, body, 0)
+        lax.fori_loop(h * HALF, (h + 1) * HALF, body, 0, unroll=2)
 
     lacc[...] = jnp.zeros_like(lacc)
     select(0)
@@ -516,23 +539,20 @@
     past = (lrow < REQ * SUF) & (llane // 2 == lrow // SUF) & (lrow % SUF < length)
     fresh_row = lrow - REQ * SUF
     fresh = (
-        (fresh_row >= 0)
-        & (fresh_row < 2 * REQ)
-        & (llane // 2 == fresh_row // 2)
-        & (fresh_row % 2 <= llane % 2)
+        (fresh_row >= 0) & (llane // 2 == fresh_row // 16) & (fresh_row % 16 <= llane % 2)
     )
     lbias[...] = jnp.where((llane < 2 * REQ) & ~(past | fresh), DROP, 0.0).astype(jnp.bfloat16)
     lpick[...] = jnp.where(lane == row // 8, 1.0, 0.0).astype(jnp.bfloat16)
-    blank = jnp.zeros((LOCAL - REQ * SUF - 2 * REQ, KV * HEAD), jnp.bfloat16)
     for cache, new in ((sk, nk_ref), (sv, nv_ref)):
-        cache[pl.ds(REQ * SUF, 2 * REQ), :] = new[...]
-        cache[pl.ds(REQ * SUF + 2 * REQ, LOCAL - REQ * SUF - 2 * REQ), :] = blank
+        cache[pl.ds(REQ * SUF, 16 * REQ), :] = jnp.zeros((16 * REQ, KV * HEAD), jnp.bfloat16)
+        for r in range(REQ):
+            cache[pl.ds(REQ * SUF + 16 * r, 2), :] = new[r]
 
     for load in loads[2:]:
         load.wait()
     meta_waited = False
 
-    waiting = [0]
+    waiting = (0,)
     for s in range(1, zh + 1):
         blocks = (nz - s, s) if s < zh else (zh,)
         for h in range(2):
@@ -555,17 +575,15 @@
                     nrecv_sem.at[step],
                     at_x(step),
                 )
-        for b in waiting:
-            serve(b)
-        waiting = list(blocks)
+        serve(waiting)
+        waiting = blocks
     for s in range(zh + 1, yh + 1):
         for b in (ny - s, s) if s < yh else (yh,):
             root_arrived(b)
             forward_root(b)
             share_root(b)
 
-    for b in waiting:
-        serve(b)
+    serve(waiting)
     give_back(zh)
     order = [(zh,)] + [(s, nz - s) for s in range(zh - 1, 0, -1)] + [(0,)]
     for b in order[1]:
@@ -573,21 +591,19 @@
 
     for b in range(ny):
         arrived(rkv.at[ny + b], cs_sem.at[b], cr_sem.at[b], sibling)
-    per_turn = -(-KV // zh)
-    done = 0
+    shares = [KV * (turn + 1) // zh for turn in range(zh)]
     for turn, blocks in enumerate(order[:-1]):
+        if turn == 0:
+            attend_local(0, shares[0])
         for b in blocks:
             answers_arrived(b)
         for h in range(2):
-            for b in blocks:
-                combine(b, h)
+            combine(blocks, h)
         if turn + 2 < len(order):
             for b in order[turn + 2]:
                 give_back(b)
-        upto = min(KV, done + per_turn)
-        if done < upto:
-            attend_local(done, upto)
-        done = upto
+        if turn:
+            attend_local(shares[turn - 1], shares[turn])
     answers_arrived(0)
     for h in range(2):
         finish(h)
@@ -657,7 +673,8 @@
             pltpu.VMEM((KV, ROWS, HEAD), f32),
             pltpu.VMEM((KV, ROWS, HEAD), f32),
             pltpu.VMEM((KV, ROWS, HEAD), f32),
-            pltpu.VMEM((ROWS, ROWS), f32),
+            pltpu.VMEM((2, ROWS, ROWS), f32),
+            pltpu.VMEM((nz, ROWS, ROWS), f32),
             dma((6,)),
             dma((nz, 2)),
             dma((nz, 2)),
@@ -681,7 +698,7 @@
             dma((ny,)),
         ],
         compiler_params=pltpu.CompilerParams(
-            collective_id=0, has_side_effects=True, vmem_limit_bytes=48 * 1024 * 1024
+            collective_id=0, has_side_effects=True, vmem_limit_bytes=60 * 1024 * 1024 + 512 * 1024
         ),
         cost_estimate=pl.CostEstimate(
             flops=4_000_000_000, bytes_accessed=5_000_000, transcendentals=8_000_000
@@ -689,8 +706,8 @@
         name="shared_prefix_attention",
     )(
         head_major,
-        new_keys.reshape(2 * REQ, width),
-        new_values.reshape(2 * REQ, width),
+        new_keys,
+        new_values,
         suffix_keys.reshape(REQ * SUF, width),
         suffix_values.reshape(REQ * SUF, width),
         root_keys,
@@ -700,7 +717,7 @@
         suffix_lengths,
         prefix_lengths,
         owner_map,
-        block_lists,
+        block_lists.T,
     )
     return out.reshape(KV, REQ, 2, 8, HEAD).transpose(1, 2, 0, 3, 4).reshape(REQ, 2, 64 * HEAD)
 

time: 113 us -> 90.6 us (0.80)
  Pallas kernels: 103 us -> 86.7 us
  local copies, waits for them, and re-layouts: 9.46 us -> 3.69 us
    pallas_call x1, Pallas kernels: 103 us -> 86.7 us  [shards(): pl.pallas_call(functools.partial(kernel, nz, ny), out_shape=jax.ShapeDtyp...]
    unnamed x19 -> x0, local copies, waits for them, and re-layouts: 5.87 us -> none
    reshape x2 -> x0, local copies, waits for them, and re-layouts: 1.55 us -> none  [the longest x1 0.78 us: shards(): new_values.reshape(2 * REQ, width)]
where the time goes in v2:
time: 90.6 us; the launch traced here: 90.4 us
  Pallas kernels  86.7 us (96%)
  local copies, waits for them, and re-layouts  3.69 us (4%)
    pallas_call x1, Pallas kernels, shards(): pl.pallas_call(functools.partial(kernel, nz, ny), out_shape=jax.ShapeDtyp...  86.7 us
    reshape x2, local copies, waits for them, and re-layouts, shards(): queries.reshape(REQ, 2, KV, 8, HEAD).transpose(2, 0, 1, 3, 4)  1.91 us

profile of v2, /device:TPU:24, one launch (start us, length us, event | category | flops | bytes accessed | tf_op | source)
XLA Modules:
  0.0 90.4 jit_solution(8960984842849895702)
XLA Ops:
  0.0 1.2 %reshape.24 = bf16[8,2,8,8,128]{4,3,2,1,0:T(8,128)(2,1)S(1)} reshape(bf16[8,2,8192]{2,1,0:T(2,128)(2,1)} %param.13) | data formatting | bytes 524288 | tf_op jit(solution)/shard_map/reshape | solution.py:633
  1.2 0.8 copy.14
  1.9 86.7 %shared_prefix_attention.1 = bf16[8,128,128]{2,1,0:T(8,128)(2,1)} custom-call(bf16[8,128,128]{2,1,0:T(8,128)(2,1)} %bitcast.13, bf16[8,2,1024]{2,1,0:T(2,128)(2,1)} %nk_ref.1, bf16[8,2,1024]{2,1,0:T(2,128)(2,1)} %nv_ref.1, bf16[256,1024]{1,0:T(8,128)(2,1)} %bitcast.17, bf16[256,1024]{1,0:T(8,128)(2,1)} %bitcast.18, bf16[64,1024]{1,0:T(8,128)(2,1)} %rk_ref.1, ...), custom_call_target="tpu_custom_call" | custom-call | flops 4000000000 | bytes 5000000 | tf_op jit(solution)/shard_map/shared_prefix_attention/pallas_call | solution.py:642
  88.6 1.0 %copy.15 = bf16[8,2,8,8,128]{4,3,2,1,0:T(8,128)(2,1)S(1)} copy(bf16[8,2,8,8,128]{4,3,1,0,2:T(8,128)(2,1)} %bitcast.14) | data formatting | bytes 524288 | tf_op jit(solution)/shard_map/transpose | solution.py:722
  89.6 0.8 reshape.31

commit v3 on v2

--- a/solution.py
+++ b/solution.py
@@ -79,27 +79,18 @@
     loc_tot,
     lacc,
     second_slot,
+    score_even,
+    score_odd,
     local_sem,
-    zs_sem,
+    sent_sem,
+    all_sem,
     zr_sem,
-    ms_sem,
-    mr_sem,
-    nsend_sem,
-    nrecv_sem,
-    xs_sem,
     xr_sem,
-    bs_sem,
     br_sem,
-    ls_sem,
     lr_sem,
-    rs_sem,
     rr_sem,
-    es_sem,
     er_sem,
-    ys_sem,
     yr_sem,
-    cs_sem,
-    cr_sem,
 ):
     zh = nz // 2
     yh = ny // 2
@@ -118,29 +109,19 @@
         return (lax.rem(y + step + ny, ny) * CORES + core, dev)
 
     sibling = (y * CORES + 1 - core, dev)
-    drains = []
 
     def send(src, dst, send_sem, recv_sem, device):
-        copy = pltpu.make_async_remote_copy(
+        pltpu.make_async_remote_copy(
             src_ref=src,
             dst_ref=dst,
             send_sem=send_sem,
             recv_sem=recv_sem,
             device_id=device,
             device_id_type=MESH,
-        )
-        copy.start()
-        drains.append(copy)
-
-    def arrived(ref, send_sem, recv_sem, device):
-        pltpu.make_async_remote_copy(
-            src_ref=ref,
-            dst_ref=ref,
-            send_sem=send_sem,
-            recv_sem=recv_sem,
-            device_id=device,
-            device_id_type=MESH,
-        ).wait_recv()
+        ).start()
+
+    def arrived(ref, recv_sem):
+        pltpu.make_async_copy(ref, ref, recv_sem).wait()
 
     loads = [
         pltpu.make_async_copy(rk_ref, rkv.at[0, 0], local_sem.at[0]),
@@ -185,7 +166,7 @@
         send(
             q_half(b, h),
             zq.at[into, pl.ds(h * HALF, HALF)],
-            zs_sem.at[into, h],
+            sent_sem.at[0],
             zr_sem.at[into, h],
             at_z(step),
         )
@@ -201,9 +182,7 @@
                 pass_queries(b, h, step, into)
 
     def query_arrived(b, h):
-        arrived(
-            zq.at[b, pl.ds(h * HALF, HALF)], zs_sem.at[b, h], zr_sem.at[b, h], at_z(1)
-        )
+        arrived(zq.at[b, pl.ds(h * HALF, HALF)], zr_sem.at[b, h])
 
     for h in range(2):
         forward_queries(0, h)
@@ -211,8 +190,8 @@
         send(
             metaz.at[0],
             metaz.at[(-step) % nz],
-            ms_sem.at[step],
-            mr_sem.at[(-step) % nz],
+            sent_sem.at[1],
+            all_sem.at[0],
             at_z(step),
         )
 
@@ -220,7 +199,7 @@
     loads[1].wait()
 
     def share_root(b):
-        send(rkv.at[b], rkv.at[ny + b], cs_sem.at[b], cr_sem.at[b], sibling)
+        send(rkv.at[b], rkv.at[ny + b], sent_sem.at[2], all_sem.at[1], sibling)
 
     def forward_root(b):
         for step in (1, -1):
@@ -233,7 +212,7 @@
                     send(
                         rkv.at[b, part],
                         rkv.at[into, part],
-                        ys_sem.at[into, part],
+                        sent_sem.at[3],
                         yr_sem.at[into, part],
                         at_y(step),
                     )
@@ -241,7 +220,7 @@
                     send(
                         rkv.at[b],
                         rkv.at[into],
-                        ys_sem.at[into, 0],
+                        sent_sem.at[3],
                         yr_sem.at[into, 0],
                         at_y(step),
                     )
@@ -249,9 +228,9 @@
     def root_arrived(b):
         if b == yh:
             for part in range(2):
-                arrived(rkv.at[b, part], ys_sem.at[b, part], yr_sem.at[b, part], at_y(1))
+                arrived(rkv.at[b, part], yr_sem.at[b, part])
         else:
-            arrived(rkv.at[b], ys_sem.at[b, 0], yr_sem.at[b, 0], at_y(1))
+            arrived(rkv.at[b], yr_sem.at[b, 0])
 
     forward_root(0)
     share_root(0)
@@ -261,14 +240,22 @@
     same_place = row % 16 == lane % 16
     diagonal = jnp.where(row == lane, 0.0, DROP)
 
-    def select(b):
+    def there(step):
+        return pl.ds(pl.multiple_of(lax.rem(x + step, NX) * SLOT_ROWS, SLOT_ROWS), SLOT_ROWS)
+
+    mine = there(0)
+    others = pl.ds(0, (NX - 1) * SLOT_ROWS)
+
+    def route(b):
         wanted = z * (2 * NX) + row // 16
         first = metaz[b, pl.ds(0, 1), :] // 2
         second = metaz[b, pl.ds(1, 1), :] // 2
         hit = ((first == wanted) | (second == wanted)) & same_place
         onehot[b] = jnp.where(hit, 1.0, 0.0).astype(jnp.bfloat16)
         bias_t[b] = jnp.where(hit, 0.0, DROP).T
-        mine = pl.ds(pl.multiple_of(x * SLOT_ROWS, SLOT_ROWS), SLOT_ROWS)
+
+    def select(b, h):
+        part = pl.ds(h * HALF, HALF)
 
         def body(k, carry):
             block = q_ref[k] if b == 0 else zq[b, k]
@@ -276,56 +263,57 @@
             snd[b, k] = chosen.astype(jnp.bfloat16)
             return carry
 
-        lax.fori_loop(0, KV, body, 0, unroll=4)
+        lax.fori_loop(h * HALF, (h + 1) * HALF, body, 0, unroll=True)
+        for step in range(1, NX):
+            send(
+                snd.at[b, part, there(step), :],
+                rcv.at[b, part, mine, :],
+                sent_sem.at[4],
+                xr_sem.at[b, h],
+                at_x(step),
+            )
 
         def keep(k, carry):
             rcv[b, k, mine, :] = snd[b, k, mine, :]
             return carry
 
-        lax.fori_loop(0, KV, keep, 0, unroll=True)
-        for step in range(1, NX):
-            there = pl.ds(pl.multiple_of(lax.rem(x + step, NX) * SLOT_ROWS, SLOT_ROWS), SLOT_ROWS)
-            send(
-                snd.at[b, :, there, :],
-                rcv.at[b, :, mine, :],
-                xs_sem.at[b, NX - step],
-                xr_sem.at[b, NX - step],
-                at_x(step),
-            )
-
-    def slots_arrived(b):
-        for step in range(1, NX):
-            there = pl.ds(pl.multiple_of(lax.rem(x + step, NX) * SLOT_ROWS, SLOT_ROWS), SLOT_ROWS)
-            arrived(
-                rcv.at[b, :, there, :], xs_sem.at[b, step], xr_sem.at[b, step], at_x(step)
-            )
+        lax.fori_loop(h * HALF, (h + 1) * HALF, keep, 0, unroll=True)
+
+    def slots_arrived(b, h):
+        arrived(rcv.at[b, pl.ds(h * HALF, HALF), others, :], xr_sem.at[b, h])
 
     ones_prefix = jnp.ones((BLK, HEAD), jnp.bfloat16)
 
-    def serve(blocks):
-        for b in blocks:
-            slots_arrived(b)
-            for source in range(NX):
-                code = metax[source, b]
-                srow = iota((SLOT_ROWS, ROWS), 0)
-                slane = iota((SLOT_ROWS, ROWS), 1)
-                wanted = (dev * 2 + srow // 16) * 2 + 1
-                hit = (code[0:1, :] == wanted) | (code[1:2, :] == wanted)
-                second = jnp.max(jnp.where(hit, 1.0, 0.0), axis=1, keepdims=True)
-                here = pl.ds(source * SLOT_ROWS, SLOT_ROWS)
-                pick[b, here, :] = jnp.where(
-                    slane == 0, 1.0 - second, jnp.where(slane == 1, second, 0.0)
-                ).astype(jnp.bfloat16)
-                second_slot[b, here, :] = jnp.broadcast_to(second, (SLOT_ROWS, ROWS))
-
-        def body(k, carry):
+    def label_slots(b):
+        for source in range(NX):
+            code = metax[source, b]
+            srow = iota((SLOT_ROWS, ROWS), 0)
+            slane = iota((SLOT_ROWS, ROWS), 1)
+            wanted = (dev * 2 + srow // 16) * 2 + 1
+            hit = (code[0:1, :] == wanted) | (code[1:2, :] == wanted)
+            second = jnp.max(jnp.where(hit, 1.0, 0.0), axis=1, keepdims=True)
+            here = pl.ds(source * SLOT_ROWS, SLOT_ROWS)
+            pick[b, here, :] = jnp.where(
+                slane == 0, 1.0 - second, jnp.where(slane == 1, second, 0.0)
+            ).astype(jnp.bfloat16)
+            second_slot[b, here, :] = jnp.broadcast_to(second, (SLOT_ROWS, ROWS))
+
+    def serve(blocks, halves):
+        rows = len(blocks) * ROWS
+        last = HALF * (halves[-1] + 1) - 1
+
+        def score(k, into):
             cols = pl.ds(pl.multiple_of(k * HEAD, HEAD), HEAD)
             queries = jnp.concatenate(
                 [jnp.concatenate([rcv[b, k], pick[b]], axis=1) for b in blocks], axis=0
             )
             keys = jnp.concatenate([pk[:, cols], kbias[...]], axis=1)
             both = lax.dot_general(queries, keys, NT, preferred_element_type=jnp.float32)
-            scores = jnp.maximum(both[:, :BLK], both[:, BLK:])
+            into[pl.ds(0, rows), :] = jnp.maximum(both[:, :BLK], both[:, BLK:])
+
+        def weigh(k, source):
+            cols = pl.ds(pl.multiple_of(k * HEAD, HEAD), HEAD)
+            scores = source[pl.ds(0, rows), :]
             highest = jnp.max(scores, axis=1, keepdims=True)
             weights = jnp.exp2((scores - highest) * SCALE2).astype(jnp.bfloat16)
             values = jnp.concatenate([pv[:BLK, cols], pv[BLK:, cols], ones_prefix], axis=1)
@@ -340,28 +328,37 @@
                 )
                 ans[b, k] = (chosen * inverse[part]).astype(jnp.bfloat16)
                 lacc[at] = jnp.where(lane == k, logs[part], lacc[at])
+
+        def body(turn, carry):
+            k = HALF * halves[0] + 2 * turn
+            score(k + 1, score_odd)
+            weigh(k, score_even)
+            score(jnp.minimum(k + 2, last), score_even)
+            weigh(k + 1, score_odd)
             return carry
 
-        lax.fori_loop(0, KV, body, 0, unroll=2)
+        score(HALF * halves[0], score_even)
+        lax.fori_loop(0, len(halves) * HALF // 2, body, 0)
         for at, b in enumerate(blocks):
-            lmine[b] = lacc[at].T[:KV, :]
-
-    def give_back(b):
-        mine = pl.ds(pl.multiple_of(x * SLOT_ROWS, SLOT_ROWS), SLOT_ROWS)
+            logs = lacc[at].T[:KV, :]
+            for h in halves:
+                lmine[b, h] = logs
+
+    def give_back(b, h):
+        part = pl.ds(h * HALF, HALF)
         for step in range(1, NX):
-            there = pl.ds(pl.multiple_of(lax.rem(x + step, NX) * SLOT_ROWS, SLOT_ROWS), SLOT_ROWS)
             send(
-                ans.at[b, :, there, :],
-                ret.at[b, :, mine, :],
-                bs_sem.at[b, NX - step],
-                br_sem.at[b, NX - step],
+                ans.at[b, part, there(step), :],
+                ret.at[b, part, mine, :],
+                sent_sem.at[5],
+                br_sem.at[b, h],
                 at_x(step),
             )
             send(
-                lmine.at[b],
-                lret.at[b, NX - step],
-                ls_sem.at[b, NX - step],
-                lr_sem.at[b, NX - step],
+                lmine.at[b, h],
+                lret.at[b, h, NX - step],
+                sent_sem.at[6],
+                lr_sem.at[b, h],
                 at_x(step),
             )
 
@@ -369,20 +366,17 @@
             ret[b, k, mine, :] = ans[b, k, mine, :]
             return carry
 
-        lax.fori_loop(0, KV, body, 0, unroll=True)
-
-    def answers_arrived(b):
+        lax.fori_loop(h * HALF, (h + 1) * HALF, body, 0, unroll=True)
+
+    def answers_arrived(b, h):
         lane8 = iota((KV, ROWS), 1)
-        rows = lmine[b]
+        rows = lmine[b, h]
+        arrived(ret.at[b, pl.ds(h * HALF, HALF), others, :], br_sem.at[b, h])
+        arrived(lret.at[b, h, pl.ds(1, NX - 1)], lr_sem.at[b, h])
         for step in range(1, NX):
-            there = pl.ds(pl.multiple_of(lax.rem(x + step, NX) * SLOT_ROWS, SLOT_ROWS), SLOT_ROWS)
-            arrived(
-                ret.at[b, :, there, :], bs_sem.at[b, step], br_sem.at[b, step], at_x(step)
-            )
-            arrived(lret.at[b, step], ls_sem.at[b, step], lr_sem.at[b, step], at_x(step))
-            moved = pltpu.roll(lret[b, step], SLOT_ROWS * step, 1)
+            moved = pltpu.roll(lret[b, h, step], SLOT_ROWS * step, 1)
             rows = jnp.where(lane8 // SLOT_ROWS == lax.rem(x + step, NX), moved, rows)
-        lslot[b] = rows
+        lslot[b, h] = rows
 
     def chain(b, h):
         step = 1 if b < zh or (b == zh and h == 0) else -1
@@ -394,13 +388,8 @@
         return b != zh and (b not in (zh - 1, zh + 1) or chain(zh, h)[1] == b)
 
     def partial_arrived(place, h):
-        arrived(
-            rsin.at[place, pl.ds(h * HALF, HALF)],
-            rs_sem.at[place, h],
-            rr_sem.at[place, h],
-            at_z(1),
-        )
-        arrived(lin.at[place, h], es_sem.at[place, h], er_sem.at[place, h], at_z(1))
+        arrived(rsin.at[place, pl.ds(h * HALF, HALF)], rr_sem.at[place, h])
+        arrived(lin.at[place, h], er_sem.at[place, h])
 
     def combine(blocks, h):
         for b in blocks:
@@ -408,20 +397,28 @@
                 partial_arrived(b, h)
 
         def body(k, carry):
-            for at, b in enumerate(blocks):
-                rows = jnp.broadcast_to(lslot[b, pl.ds(k, 1), :], (ROWS, ROWS)) + bias_t[b]
-                parts = ret[b, k]
+            def logs(b):
+                rows = jnp.broadcast_to(lslot[b, h, pl.ds(k, 1), :], (ROWS, ROWS)) + bias_t[b]
                 if has_input(b, h):
                     extra = jnp.broadcast_to(lin[b, h, pl.ds(k, 1), :], (ROWS, ROWS)) + diagonal
                     rows = jnp.concatenate([rows, extra], axis=1)
+                return rows
+
+            highest = [
+                jnp.maximum(jnp.max(logs(b), axis=1, keepdims=True), FLOOR) for b in blocks
+            ]
+            weights = [jnp.exp2(logs(b) - top).astype(jnp.bfloat16) for b, top in zip(blocks, highest)]
+            sums = []
+            for b, weight in zip(blocks, weights):
+                parts = ret[b, k]
+                if has_input(b, h):
                     parts = jnp.concatenate([parts, rsin[b, k]], axis=0)
-                highest = jnp.maximum(jnp.max(rows, axis=1, keepdims=True), FLOOR)
-                weights = jnp.exp2(rows - highest).astype(jnp.bfloat16)
                 parts = jnp.concatenate([parts, jnp.ones_like(parts)], axis=1)
-                summed = jnp.dot(weights, parts, preferred_element_type=jnp.float32)
-                totals = jnp.maximum(summed[:, HEAD:], 1.0e-30)
-                rsout[b, k] = (summed[:, :HEAD] / totals).astype(jnp.bfloat16)
-                lacc[at] = jnp.where(lane == k, highest + jnp.log(totals) * LOG2E, lacc[at])
+                sums.append(jnp.dot(weight, parts, preferred_element_type=jnp.float32))
+            for at, b in enumerate(blocks):
+                totals = jnp.maximum(sums[at][:, HEAD:], 1.0e-30)
+                rsout[b, k] = (sums[at][:, :HEAD] / totals).astype(jnp.bfloat16)
+                lacc[at] = jnp.where(lane == k, highest[at] + jnp.log(totals) * LOG2E, lacc[at])
             return carry
 
         lax.fori_loop(h * HALF, (h + 1) * HALF, body, 0, unroll=2)
@@ -432,14 +429,14 @@
             send(
                 rsout.at[b, part],
                 rsin.at[place, part],
-                rs_sem.at[place, h],
+                sent_sem.at[7],
                 rr_sem.at[place, h],
                 at_z(step),
             )
             send(
                 lout.at[b, h],
                 lin.at[place, h],
-                es_sem.at[place, h],
+                sent_sem.at[8],
                 er_sem.at[place, h],
                 at_z(step),
             )
@@ -489,7 +486,7 @@
         def body(k, carry):
             rows = jnp.concatenate(
                 [
-                    jnp.broadcast_to(lslot[0, pl.ds(k, 1), :], (ROWS, ROWS)) + bias_t[0],
+                    jnp.broadcast_to(lslot[0, h, pl.ds(k, 1), :], (ROWS, ROWS)) + bias_t[0],
                     jnp.broadcast_to(lin[0, h, pl.ds(k, 1), :], (ROWS, ROWS)) + diagonal,
                     jnp.broadcast_to(lin[zh, h, pl.ds(k, 1), :], (ROWS, ROWS)) + diagonal,
                 ],
@@ -510,16 +507,17 @@
         lax.fori_loop(h * HALF, (h + 1) * HALF, body, 0, unroll=2)
 
     lacc[...] = jnp.zeros_like(lacc)
-    select(0)
-
-    for b in range(1, nz):
-        arrived(metaz.at[b], ms_sem.at[b], mr_sem.at[b], at_z(1))
+    route(0)
+    for h in range(2):
+        select(0, h)
+
+    arrived(metaz.at[pl.ds(1, nz - 1)], all_sem.at[0])
     for step in range(1, NX):
         send(
             metaz,
             metax.at[x],
-            nsend_sem.at[NX - step],
-            nrecv_sem.at[NX - step],
+            sent_sem.at[9],
+            all_sem.at[2],
             at_x(step),
         )
     metax[x] = metaz[...]
@@ -550,7 +548,14 @@
 
     for load in loads[2:]:
         load.wait()
-    meta_waited = False
+    for b in range(1, nz):
+        route(b)
+
+    def advance_root(s):
+        for b in (ny - s, s) if s < yh else (yh,):
+            root_arrived(b)
+            forward_root(b)
+            share_root(b)
 
     waiting = (0,)
     for s in range(1, zh + 1):
@@ -559,57 +564,63 @@
             for b in blocks:
                 query_arrived(b, h)
                 forward_queries(b, h)
-        for b in blocks:
-            select(b)
+            for b in blocks:
+                select(b, h)
         if s <= yh:
-            for b in (ny - s, s) if s < yh else (yh,):
-                root_arrived(b)
-                forward_root(b)
-                share_root(b)
-        if not meta_waited:
-            meta_waited = True
-            for step in range(1, NX):
-                arrived(
-                    metax.at[lax.rem(x + step, NX)],
-                    nsend_sem.at[step],
-                    nrecv_sem.at[step],
-                    at_x(step),
-                )
-        serve(waiting)
+            advance_root(s)
+        if s == 1:
+            arrived(metax.at[pl.ds(0, NX - 1)], all_sem.at[2])
+            for b in range(nz):
+                label_slots(b)
+        for b in waiting:
+            for h in range(2):
+                slots_arrived(b, h)
+        serve(waiting, (0, 1))
         waiting = blocks
     for s in range(zh + 1, yh + 1):
-        for b in (ny - s, s) if s < yh else (yh,):
-            root_arrived(b)
-            forward_root(b)
-            share_root(b)
-
-    serve(waiting)
-    give_back(zh)
+        advance_root(s)
+
     order = [(zh,)] + [(s, nz - s) for s in range(zh - 1, 0, -1)] + [(0,)]
-    for b in order[1]:
-        give_back(b)
-
-    for b in range(ny):
-        arrived(rkv.at[ny + b], cs_sem.at[b], cr_sem.at[b], sibling)
+    for h in range(2):
+        slots_arrived(zh, h)
+        serve((zh,), (h,))
+        give_back(zh, h)
+
+    arrived(rkv.at[pl.ds(ny, ny)], all_sem.at[1])
     shares = [KV * (turn + 1) // zh for turn in range(zh)]
+    attend_local(0, shares[0])
     for turn, blocks in enumerate(order[:-1]):
-        if turn == 0:
-            attend_local(0, shares[0])
-        for b in blocks:
-            answers_arrived(b)
         for h in range(2):
+            if turn == 0:
+                for b in order[1]:
+                    give_back(b, h)
+            for b in blocks:
+                answers_arrived(b, h)
             combine(blocks, h)
-        if turn + 2 < len(order):
-            for b in order[turn + 2]:
-                give_back(b)
+            if turn + 2 < len(order):
+                for b in order[turn + 2]:
+                    give_back(b, h)
         if turn:
             attend_local(shares[turn - 1], shares[turn])
-    answers_arrived(0)
     for h in range(2):
+        answers_arrived(0, h)
         finish(h)
 
-    for copy in drains:
-        copy.wait_send()
+    for at, ref in enumerate(
+        (
+            zq.at[pl.ds(1, nz - 1)],
+            metaz.at[pl.ds(1, nz - 1)],
+            rkv.at[pl.ds(0, ny)],
+            rkv.at[pl.ds(1, ny - 1)],
+            rcv.at[:, :, others, :],
+            ret.at[:, :, others, :],
+            lret.at[:, :, pl.ds(1, NX - 1)],
+            rsin.at[pl.ds(1, nz - 1)],
+            lin.at[pl.ds(1, nz - 1)],
+            metax.at[pl.ds(1, NX - 1)],
+        )
+    ):
+        arrived(ref, sent_sem.at[at])
 
 
 def shards(nz, ny, *args):
@@ -665,9 +676,9 @@
             pltpu.VMEM((2 * BLK, HEAD), bf16),
             pltpu.VMEM((LOCAL, HEAD), bf16),
             pltpu.VMEM((ROWS, HEAD), bf16),
-            pltpu.VMEM((nz, KV, ROWS), f32),
-            pltpu.VMEM((nz, NX, KV, ROWS), f32),
-            pltpu.VMEM((nz, KV, ROWS), f32),
+            pltpu.VMEM((nz, 2, KV, ROWS), f32),
+            pltpu.VMEM((nz, 2, NX, KV, ROWS), f32),
+            pltpu.VMEM((nz, 2, KV, ROWS), f32),
             pltpu.VMEM((nz, 2, KV, ROWS), f32),
             pltpu.VMEM((nz, 2, KV, ROWS), f32),
             pltpu.VMEM((KV, ROWS, HEAD), f32),
@@ -675,27 +686,18 @@
             pltpu.VMEM((KV, ROWS, HEAD), f32),
             pltpu.VMEM((2, ROWS, ROWS), f32),
             pltpu.VMEM((nz, ROWS, ROWS), f32),
+            pltpu.VMEM((2 * ROWS, BLK), f32),
+            pltpu.VMEM((2 * ROWS, BLK), f32),
             dma((6,)),
+            dma((10,)),
+            dma((3,)),
             dma((nz, 2)),
             dma((nz, 2)),
-            dma((nz,)),
-            dma((nz,)),
-            dma((NX,)),
-            dma((NX,)),
-            dma((nz, NX)),
-            dma((nz, NX)),
-            dma((nz, NX)),
-            dma((nz, NX)),
-            dma((nz, NX)),
-            dma((nz, NX)),
             dma((nz, 2)),
             dma((nz, 2)),
             dma((nz, 2)),
             dma((nz, 2)),
             dma((ny, 2)),
-            dma((ny, 2)),
-            dma((ny,)),
-            dma((ny,)),
         ],
         compiler_params=pltpu.CompilerParams(
             collective_id=0, has_side_effects=True, vmem_limit_bytes=60 * 1024 * 1024 + 512 * 1024

time: 90.6 us -> 87.1 us (0.961)
  the two profiles are of different devices: /device:TPU:24 before, /device:TPU:16 now
where the time goes in v3:
time: 87.1 us; the launch traced here: 86.9 us
  Pallas kernels  83.2 us (96%)
  local copies, waits for them, and re-layouts  3.69 us (4%)
    pallas_call x1, Pallas kernels, shards(): pl.pallas_call(functools.partial(kernel, nz, ny), out_shape=jax.ShapeDtyp...  83.2 us
    reshape x2, local copies, waits for them, and re-layouts, shards(): queries.reshape(REQ, 2, KV, 8, HEAD).transpose(2, 0, 1, 3, 4)  1.91 us

profile of v3, /device:TPU:16, one launch (start us, length us, event | category | flops | bytes accessed | tf_op | source)
XLA Modules:
  0.0 86.9 jit_solution(5489403884975320678)
XLA Ops:
  0.0 1.2 %reshape.24 = bf16[8,2,8,8,128]{4,3,2,1,0:T(8,128)(2,1)S(1)} reshape(bf16[8,2,8192]{2,1,0:T(2,128)(2,1)} %param.13) | data formatting | bytes 524288 | tf_op jit(solution)/shard_map/reshape | solution.py:644
  1.2 0.8 copy.14
  1.9 83.2 %shared_prefix_attention.1 = bf16[8,128,128]{2,1,0:T(8,128)(2,1)} custom-call(bf16[8,128,128]{2,1,0:T(8,128)(2,1)} %bitcast.13, bf16[8,2,1024]{2,1,0:T(2,128)(2,1)} %nk_ref.1, bf16[8,2,1024]{2,1,0:T(2,128)(2,1)} %nv_ref.1, bf16[256,1024]{1,0:T(8,128)(2,1)} %bitcast.17, bf16[256,1024]{1,0:T(8,128)(2,1)} %bitcast.18, bf16[64,1024]{1,0:T(8,128)(2,1)} %rk_ref.1, ...), custom_call_target="tpu_custom_call" | custom-call | flops 4000000000 | bytes 5000000 | tf_op jit(solution)/shard_map/shared_prefix_attention/pallas_call | solution.py:653
  85.1 1.0 %copy.15 = bf16[8,2,8,8,128]{4,3,2,1,0:T(8,128)(2,1)S(1)} copy(bf16[8,2,8,8,128]{4,3,1,0,2:T(8,128)(2,1)} %bitcast.14) | data formatting | bytes 524288 | tf_op jit(solution)/shard_map/transpose | solution.py:724
  86.1 0.8 reshape.31

commit v4 on v3

--- a/solution.py
+++ b/solution.py
@@ -184,8 +184,6 @@
     def query_arrived(b, h):
         arrived(zq.at[b, pl.ds(h * HALF, HALF)], zr_sem.at[b, h])
 
-    for h in range(2):
-        forward_queries(0, h)
     for step in range(1, nz):
         send(
             metaz.at[0],
@@ -194,6 +192,9 @@
             all_sem.at[0],
             at_z(step),
         )
+
+    for h in range(2):
+        forward_queries(0, h)
 
     loads[0].wait()
     loads[1].wait()
@@ -511,17 +512,6 @@
     for h in range(2):
         select(0, h)
 
-    arrived(metaz.at[pl.ds(1, nz - 1)], all_sem.at[0])
-    for step in range(1, NX):
-        send(
-            metaz,
-            metax.at[x],
-            sent_sem.at[9],
-            all_sem.at[2],
-            at_x(step),
-        )
-    metax[x] = metaz[...]
-
     prow = iota((2 * BLK, HEAD), 0)
     plane = iota((2 * BLK, HEAD), 1)
     limit = jnp.where(prow < BLK, plen_ref[0], plen_ref[1])
@@ -548,8 +538,17 @@
 
     for load in loads[2:]:
         load.wait()
-    for b in range(1, nz):
-        route(b)
+    def exchange_routes():
+        arrived(metaz.at[pl.ds(1, nz - 1)], all_sem.at[0])
+        for step in range(1, NX):
+            send(
+                metaz,
+                metax.at[x],
+                sent_sem.at[9],
+                all_sem.at[2],
+                at_x(step),
+            )
+        metax[x] = metaz[...]
 
     def advance_root(s):
         for b in (ny - s, s) if s < yh else (yh,):
@@ -557,28 +556,42 @@
             forward_root(b)
             share_root(b)
 
-    waiting = (0,)
+    def serve_step(s):
+        blocks = (nz - s, s) if 0 < s < zh else (s,)
+        for b in blocks:
+            label_slots(b)
+            for h in range(2):
+                slots_arrived(b, h)
+        serve(blocks, (0, 1))
+
+    served = 0
     for s in range(1, zh + 1):
         blocks = (nz - s, s) if s < zh else (zh,)
         for h in range(2):
             for b in blocks:
                 query_arrived(b, h)
                 forward_queries(b, h)
+        if s == 1:
+            exchange_routes()
+        for b in blocks:
+            route(b)
+        for h in range(2):
             for b in blocks:
                 select(b, h)
-        if s <= yh:
+        if s == min(2, zh):
+            arrived(metax.at[pl.ds(0, NX - 1)], all_sem.at[2])
+        while served < s - 1:
+            serve_step(served)
+            served += 1
+        if s < min(zh, yh):
             advance_root(s)
-        if s == 1:
-            arrived(metax.at[pl.ds(0, NX - 1)], all_sem.at[2])
-            for b in range(nz):
-                label_slots(b)
-        for b in waiting:
-            for h in range(2):
-                slots_arrived(b, h)
-        serve(waiting, (0, 1))
-        waiting = blocks
-    for s in range(zh + 1, yh + 1):
-        advance_root(s)
+        if s == zh - 1 and s > 1:
+            serve_step(served)
+            served += 1
+    while served < zh:
+        serve_step(served)
+        served += 1
+    label_slots(zh)
 
     order = [(zh,)] + [(s, nz - s) for s in range(zh - 1, 0, -1)] + [(0,)]
     for h in range(2):
@@ -586,21 +599,25 @@
         serve((zh,), (h,))
         give_back(zh, h)
 
-    arrived(rkv.at[pl.ds(ny, ny)], all_sem.at[1])
-    shares = [KV * (turn + 1) // zh for turn in range(zh)]
-    attend_local(0, shares[0])
+    for s in range(min(zh, yh), yh + 1):
+        advance_root(s)
+    shares = [-(-KV * turn // (zh - 1)) for turn in range(zh)]
+    for b in order[1]:
+        give_back(b, 0)
     for turn, blocks in enumerate(order[:-1]):
         for h in range(2):
-            if turn == 0:
-                for b in order[1]:
-                    give_back(b, h)
             for b in blocks:
                 answers_arrived(b, h)
+            if turn == 0:
+                ahead = [(b, 1) for b in order[1]] if h == 0 else []
+            else:
+                ahead = [(b, h) for b in order[turn + 1]]
+            for b, part in ahead:
+                give_back(b, part)
             combine(blocks, h)
-            if turn + 2 < len(order):
-                for b in order[turn + 2]:
-                    give_back(b, h)
-        if turn:
+        if turn == 0:
+            arrived(rkv.at[pl.ds(ny, ny)], all_sem.at[1])
+        else:
             attend_local(shares[turn - 1], shares[turn])
     for h in range(2):
         answers_arrived(0, h)

time: 87.1 us -> 82.7 us (0.949)
  the two profiles are of different devices: /device:TPU:16 before, /device:TPU:24 now
where the time goes in v4:
time: 82.7 us; the launch traced here: 82.5 us
  Pallas kernels  78.8 us (95%)
  local copies, waits for them, and re-layouts  3.69 us (4%)
    pallas_call x1, Pallas kernels, shards(): pl.pallas_call(functools.partial(kernel, nz, ny), out_shape=jax.ShapeDtyp...  78.8 us
    reshape x2, local copies, waits for them, and re-layouts, shards(): queries.reshape(REQ, 2, KV, 8, HEAD).transpose(2, 0, 1, 3, 4)  1.91 us

profile of v4, /device:TPU:24, one launch (start us, length us, event | category | flops | bytes accessed | tf_op | source)
XLA Modules:
  0.0 82.5 jit_solution(16398107319732782229)
XLA Ops:
  0.0 1.2 %reshape.24 = bf16[8,2,8,8,128]{4,3,2,1,0:T(8,128)(2,1)S(1)} reshape(bf16[8,2,8192]{2,1,0:T(2,128)(2,1)} %param.13) | data formatting | bytes 524288 | tf_op jit(solution)/shard_map/reshape | solution.py:661
  1.2 0.8 copy.14
  1.9 78.8 %shared_prefix_attention.1 = bf16[8,128,128]{2,1,0:T(8,128)(2,1)} custom-call(bf16[8,128,128]{2,1,0:T(8,128)(2,1)} %bitcast.13, bf16[8,2,1024]{2,1,0:T(2,128)(2,1)} %nk_ref.1, bf16[8,2,1024]{2,1,0:T(2,128)(2,1)} %nv_ref.1, bf16[256,1024]{1,0:T(8,128)(2,1)} %bitcast.17, bf16[256,1024]{1,0:T(8,128)(2,1)} %bitcast.18, bf16[64,1024]{1,0:T(8,128)(2,1)} %rk_ref.1, ...), custom_call_target="tpu_custom_call" | custom-call | flops 4000000000 | bytes 5000000 | tf_op jit(solution)/shard_map/shared_prefix_attention/pallas_call | solution.py:670
  80.7 1.0 %copy.15 = bf16[8,2,8,8,128]{4,3,2,1,0:T(8,128)(2,1)S(1)} copy(bf16[8,2,8,8,128]{4,3,1,0,2:T(8,128)(2,1)} %bitcast.14) | data formatting | bytes 524288 | tf_op jit(solution)/shard_map/transpose | solution.py:741
  81.7 0.8 reshape.31

commit v5 on v4

--- a/solution.py
+++ b/solution.py
@@ -35,7 +35,7 @@
 def kernel(
     nz,
     ny,
-    q_ref,
+    q_in,
     nk_ref,
     nv_ref,
     sk_ref,
@@ -49,6 +49,7 @@
     om_ref,
     bl_ref,
     out_ref,
+    q_ref,
     zq,
     snd,
     rcv,
@@ -143,6 +144,9 @@
     for partner in partners:
         pl.semaphore_signal(barrier, inc=1, device_id=partner, device_id_type=MESH)
 
+    for k in range(KV):
+        q_ref[k] = q_in[:, :, k].reshape(ROWS, HEAD)
+
     lane1 = iota((1, ROWS), 1)
     stored = [om_ref[0, bl_ref[p % 2, p // 2]] for p in range(2 * REQ)]
     owner = [s // 2 for s in stored]
@@ -502,7 +506,9 @@
             share = jnp.exp2(loc_max[k] - highest)
             numerator = summed[:, :HEAD] + loc_acc[k] * share
             denominator = summed[:, HEAD:] + loc_tot[k] * share
-            out_ref[k] = (numerator / denominator).astype(jnp.bfloat16)
+            out_ref[:, :, k] = (
+                (numerator / denominator).astype(jnp.bfloat16).reshape(REQ, 2, KV, HEAD)
+            )
             return carry
 
         lax.fori_loop(h * HALF, (h + 1) * HALF, body, 0, unroll=2)
@@ -612,9 +618,9 @@
                 ahead = [(b, 1) for b in order[1]] if h == 0 else []
             else:
                 ahead = [(b, h) for b in order[turn + 1]]
+            combine(blocks, h)
             for b, part in ahead:
                 give_back(b, part)
-            combine(blocks, h)
         if turn == 0:
             arrived(rkv.at[pl.ds(ny, ny)], all_sem.at[1])
         else:
@@ -657,9 +663,6 @@
         block_lists,
     ) = args
     width = KV * HEAD
-    head_major = (
-        queries.reshape(REQ, 2, KV, 8, HEAD).transpose(2, 0, 1, 3, 4).reshape(KV, ROWS, HEAD)
-    )
     root_rows = root_keys.shape[0]
     bf16, f32 = jnp.bfloat16, jnp.float32
     vmem = pl.BlockSpec(memory_space=pltpu.VMEM)
@@ -669,10 +672,11 @@
     blocks = (nz, KV, ROWS, HEAD)
     out = pl.pallas_call(
         functools.partial(kernel, nz, ny),
-        out_shape=jax.ShapeDtypeStruct((KV, ROWS, HEAD), bf16),
+        out_shape=jax.ShapeDtypeStruct((REQ, 2, KV, 8, HEAD), bf16),
         in_specs=[vmem, vmem, vmem] + [anywhere] * 6 + [smem] * 4,
         out_specs=vmem,
         scratch_shapes=[
+            pltpu.VMEM(blocks[1:], bf16),
             pltpu.VMEM(blocks, bf16),
             pltpu.VMEM(blocks, bf16),
             pltpu.VMEM(blocks, bf16),
@@ -724,7 +728,7 @@
         ),
         name="shared_prefix_attention",
     )(
-        head_major,
+        queries.reshape(REQ, 2, KV, 8, HEAD),
         new_keys,
         new_values,
         suffix_keys.reshape(REQ * SUF, width),
@@ -738,7 +742,7 @@
         owner_map,
         block_lists.T,
     )
-    return out.reshape(KV, REQ, 2, 8, HEAD).transpose(1, 2, 0, 3, 4).reshape(REQ, 2, 64 * HEAD)
+    return out.reshape(REQ, 2, 64 * HEAD)
 
 
 def solution(mesh):

time: 82.7 us -> 84.5 us (1.022)
  Pallas kernels: 78.8 us -> 80.7 us
    pallas_call x1, Pallas kernels: 78.8 us -> 80.7 us  [shards(): pl.pallas_call(functools.partial(kernel, nz, ny), out_shape=jax.ShapeDtyp...]
    transpose x1 -> x0, local copies, waits for them, and re-layouts: 1.01 us -> none  [shards(): out.reshape(KV, REQ, 2, 8, HEAD).transpose(1, 2, 0, 3, 4)]
    reshape x3 -> x2, local copies, waits for them, and re-layouts: 2.68 us -> 3.57 us  [the longest x1 1.86 us: shards(): queries.reshape(REQ, 2, KV, 8, HEAD)]
where the time goes in v5:
time: 84.5 us; the launch traced here: 84.3 us
  Pallas kernels  80.7 us (96%)
  local copies, waits for them, and re-layouts  3.57 us (4%)
    pallas_call x1, Pallas kernels, shards(): pl.pallas_call(functools.partial(kernel, nz, ny), out_shape=jax.ShapeDtyp...  80.7 us
    reshape x1, local copies, waits for them, and re-layouts, shards(): queries.reshape(REQ, 2, KV, 8, HEAD)  1.86 us
    reshape x1, local copies, waits for them, and re-layouts, shards(): return out.reshape(REQ, 2, 64 * HEAD)  1.72 us

profile of v5, /device:TPU:24, one launch (start us, length us, event | category | flops | bytes accessed | tf_op | source)
XLA Modules:
  0.0 84.3 jit_solution(18317783717593935848)
XLA Ops:
  0.0 1.9 %reshape.18.q_in = bf16[8,2,8,8,128]{4,3,2,1,0:T(8,128)(2,1)} reshape(bf16[8,2,8192]{2,1,0:T(2,128)(2,1)} %param.13) | data formatting | bytes 524288 | tf_op jit(solution)/shard_map/reshape | solution.py:731
  1.9 80.7 %shared_prefix_attention.1 = bf16[8,2,8,8,128]{4,3,2,1,0:T(8,128)(2,1)} custom-call(bf16[8,2,8,8,128]{4,3,2,1,0:T(8,128)(2,1)} %reshape.18.q_in, bf16[8,2,1024]{2,1,0:T(2,128)(2,1)} %nk_ref.1, bf16[8,2,1024]{2,1,0:T(2,128)(2,1)} %nv_ref.1, bf16[256,1024]{1,0:T(8,128)(2,1)} %bitcast.9, bf16[256,1024]{1,0:T(8,128)(2,1)} %bitcast.10, bf16[64,1024]{1,0:T(8,128)(2,1)} %rk_ref.1, ...), custom_call_target="tpu_custom_call" | custom-call | flops 4000000000 | bytes 5000000 | tf_op jit(solution)/shard_map/shared_prefix_attention/pallas_call | solution.py:673
  82.6 1.7 %reshape.23 = bf16[8,2,8192]{2,1,0:T(2,128)(2,1)} reshape(bf16[8,2,8,8,128]{4,3,2,1,0:T(8,128)(2,1)} %shared_prefix_attention.1) | data formatting | bytes 524288 | tf_op jit(solution)/shard_map/reshape | solution.py:745

commit v6 on v5

--- a/solution.py
+++ b/solution.py
@@ -618,9 +618,9 @@
                 ahead = [(b, 1) for b in order[1]] if h == 0 else []
             else:
                 ahead = [(b, h) for b in order[turn + 1]]
-            combine(blocks, h)
             for b, part in ahead:
                 give_back(b, part)
+            combine(blocks, h)
         if turn == 0:
             arrived(rkv.at[pl.ds(ny, ny)], all_sem.at[1])
         else:

time: 84.5 us -> 82.6 us (0.978)
  Pallas kernels: 80.7 us -> 78.8 us
    pallas_call x1, Pallas kernels: 80.7 us -> 78.8 us  [shards(): pl.pallas_call(functools.partial(kernel, nz, ny), out_shape=jax.ShapeDtyp...]
where the time goes in v6:
time: 82.6 us; the launch traced here: 82.4 us
  Pallas kernels  78.8 us (95%)
  local copies, waits for them, and re-layouts  3.57 us (4%)
    pallas_call x1, Pallas kernels, shards(): pl.pallas_call(functools.partial(kernel, nz, ny), out_shape=jax.ShapeDtyp...  78.8 us
    reshape x1, local copies, waits for them, and re-layouts, shards(): queries.reshape(REQ, 2, KV, 8, HEAD)  1.86 us
    reshape x1, local copies, waits for them, and re-layouts, shards(): return out.reshape(REQ, 2, 64 * HEAD)  1.72 us

profile of v6, /device:TPU:24, one launch (start us, length us, event | category | flops | bytes accessed | tf_op | source)
XLA Modules:
  0.0 82.4 jit_solution(12242671511182805927)
XLA Ops:
  0.0 1.9 %reshape.18.q_in = bf16[8,2,8,8,128]{4,3,2,1,0:T(8,128)(2,1)} reshape(bf16[8,2,8192]{2,1,0:T(2,128)(2,1)} %param.13) | data formatting | bytes 524288 | tf_op jit(solution)/shard_map/reshape | solution.py:731
  1.9 78.8 %shared_prefix_attention.1 = bf16[8,2,8,8,128]{4,3,2,1,0:T(8,128)(2,1)} custom-call(bf16[8,2,8,8,128]{4,3,2,1,0:T(8,128)(2,1)} %reshape.18.q_in, bf16[8,2,1024]{2,1,0:T(2,128)(2,1)} %nk_ref.1, bf16[8,2,1024]{2,1,0:T(2,128)(2,1)} %nv_ref.1, bf16[256,1024]{1,0:T(8,128)(2,1)} %bitcast.9, bf16[256,1024]{1,0:T(8,128)(2,1)} %bitcast.10, bf16[64,1024]{1,0:T(8,128)(2,1)} %rk_ref.1, ...), custom_call_target="tpu_custom_call" | custom-call | flops 4000000000 | bytes 5000000 | tf_op jit(solution)/shard_map/shared_prefix_attention/pallas_call | solution.py:673
  80.7 1.7 %reshape.23 = bf16[8,2,8192]{2,1,0:T(2,128)(2,1)} reshape(bf16[8,2,8,8,128]{4,3,2,1,0:T(8,128)(2,1)} %shared_prefix_attention.1) | data formatting | bytes 524288 | tf_op jit(solution)/shard_map/reshape | solution.py:745
